TPU v7x, 32 devices: a whole 2x2x4 slice. The times are simulated.
32 devices in a mesh: dp: 8 (over z, core), tensor: 4 (over y, x).
Axes of the slice: x: 2, y: 2, z: 4, core: 2. Of those that a mesh axis runs over, the one named last changes fastest.
Arguments:
- hidden_in: bfloat16 [16384, 1024], P(('dp', 'tensor')), may hold values from -6 to 6
- ln1_gain: bfloat16 [1024], P(('dp', 'tensor')), may hold values from 0.25 to 1.75
- ln1_bias: bfloat16 [1024], P(('dp', 'tensor')), may hold values from -1.5 to 1.5
- qkv_weight: bfloat16 [1024, 3, 1024], P('dp', None, 'tensor'), may hold values from -0.1875 to 0.1875
- qv_bias: bfloat16 [2048], P(('dp', 'tensor')), may hold values from -1.5 to 1.5
- out_weight: bfloat16 [1024, 1024], P('dp', 'tensor'), may hold values from -0.75 to 0.75
- out_bias: bfloat16 [1024], P(('dp', 'tensor')), may hold values from -1.5 to 1.5
- ln2_gain: bfloat16 [1024], P(('dp', 'tensor')), may hold values from 0.25 to 1.75
- ln2_bias: bfloat16 [1024], P(('dp', 'tensor')), may hold values from -1.5 to 1.5
- fc_weight: bfloat16 [1024, 4096], P('dp', 'tensor'), may hold values from -0.1875 to 0.1875
- fc_bias: bfloat16 [4096], P(('dp', 'tensor')), may hold values from -1.5 to 1.5
- proj_weight: bfloat16 [1024, 4096], P('dp', 'tensor'), may hold values from -0.09375 to 0.09375
- proj_bias: bfloat16 [1024], P(('dp', 'tensor')), may hold values from -1.5 to 1.5
- segment_ids: int32 [16384], P('dp'), may hold values from 0 to 1, as said below
- out_grad: bfloat16 [16384, 1024], P(('dp', 'tensor')), may hold values from -6 to 6
Outputs:
- layer_out: bfloat16 [16384, 1024], P(('dp', 'tensor'))
- in_grad: bfloat16 [16384, 1024], P(('dp', 'tensor'))
- grad_ln1_gain: float32 [1024], P(('dp', 'tensor'))
- grad_ln1_bias: float32 [1024], P(('dp', 'tensor'))
- grad_qkv_weight: float32 [1024, 3, 1024], P('dp', None, 'tensor')
- grad_qv_bias: float32 [2048], P(('dp', 'tensor'))
- grad_out_weight: float32 [1024, 1024], P('dp', 'tensor')
- grad_out_bias: float32 [1024], P(('dp', 'tensor'))
- grad_ln2_gain: float32 [1024], P(('dp', 'tensor'))
- grad_ln2_bias: float32 [1024], P(('dp', 'tensor'))
- grad_fc_weight: float32 [1024, 4096], P('dp', 'tensor')
- grad_fc_bias: float32 [4096], P(('dp', 'tensor'))
- grad_proj_weight: float32 [1024, 4096], P('dp', 'tensor')
- grad_proj_bias: float32 [1024], P(('dp', 'tensor'))
Inputs may be any that keep to these rules, and one draw needn't show every extreme that they name: `segment_ids`: each aligned block of 2048 tokens (one data group) holds whole sequences: ids start at 0 on its first token, stay equal within a sequence and rise by one at the next; each sequence has 1024 tokens or more, or the whole block where that is shorter.
All inputs are finite; a program needn't handle non-finite values.
Results may differ from a plain program's by a relative error of at most 0.02.
Values may be sent and summed in bfloat16 or wider, within the bound.
A program may use at most 384 MiB of HBM per device.

v0:
```python
import jax
import jax.numpy as jnp
from jax import lax
from jax.sharding import PartitionSpec as P

HEADS = 16
HD = 64


NEG_FILL = -1e30
EPSILON = 1e-05


def layer_norm(values, gain_vec, shift_vec):
    center = values - jnp.mean(values, axis=-1, keepdims=True)
    spread = jnp.mean(center * center, axis=-1, keepdims=True)
    return center * lax.rsqrt(spread + EPSILON) * gain_vec + shift_vec


def gelu_tanh(values):
    return jax.nn.gelu(values, approximate=True)


def contract_rows(left, right):
    return lax.dot_general(
        left, right, (((0,), (0,)), ((), ())), preferred_element_type=jnp.float32
    )


def contract_cols(left, right):
    return lax.dot_general(
        left, right, (((1,), (1,)), ((), ())), preferred_element_type=jnp.float32
    )


def block_scores(query_rows, key_rows, first_pos, query_seg, key_seg, slopes, score_scale):
    raw_scores = (
        jnp.einsum("qhe,khe->hqk", query_rows, key_rows, preferred_element_type=jnp.float32)
        * score_scale
    )
    query_pos = first_pos + jnp.arange(query_rows.shape[0], dtype=jnp.int32)
    key_pos = jnp.arange(key_rows.shape[0], dtype=jnp.int32)
    distance = (key_pos[None, :] - query_pos[:, None]).astype(jnp.float32)
    raw_scores = raw_scores + slopes[:, None, None] * distance[None]
    allowed = (query_seg[:, None] == key_seg[None, :]) & (key_pos[None, :] <= query_pos[:, None])
    return jnp.where(allowed[None], raw_scores, NEG_FILL)


def attend(query_all, key_all, value_all, segments, slopes, score_scale, block_count):
    block_rows = query_all.shape[0] // block_count
    out_blocks = []
    log_sums = []
    for block_num in range(block_count):
        first_row = block_num * block_rows
        last_row = first_row + block_rows
        masked = block_scores(
            query_all[first_row:last_row],
            key_all[:last_row],
            first_row,
            segments[first_row:last_row],
            segments[:last_row],
            slopes,
            score_scale,
        )
        row_max = jnp.max(masked, axis=-1, keepdims=True)
        exponent = jnp.exp(masked - row_max)
        row_total = jnp.sum(exponent, axis=-1, keepdims=True)
        low_probs = (exponent / row_total).astype(jnp.bfloat16)
        out_blocks.append(
            jnp.einsum(
                "hqk,khe->qhe", low_probs, value_all[:last_row], preferred_element_type=jnp.float32
            )
        )
        log_sums.append(row_max + jnp.log(row_total))
    return (jnp.concatenate(out_blocks, 0), jnp.concatenate(log_sums, 1))


def attend_back(
    query_all, key_all, value_all, segments, slopes, score_scale, block_count, log_sums, grad_out
):
    block_rows = query_all.shape[0] // block_count
    grad_query = []
    grad_key = jnp.zeros(key_all.shape, jnp.float32)
    grad_value = jnp.zeros(value_all.shape, jnp.float32)
    for block_num in range(block_count):
        first_row = block_num * block_rows
        last_row = first_row + block_rows
        masked = block_scores(
            query_all[first_row:last_row],
            key_all[:last_row],
            first_row,
            segments[first_row:last_row],
            segments[:last_row],
            slopes,
            score_scale,
        )
        probs_full = jnp.exp(masked - log_sums[:, first_row:last_row])
        low_probs = probs_full.astype(jnp.bfloat16)
        rows_grad = grad_out[first_row:last_row]
        grad_value = grad_value.at[:last_row].add(
            jnp.einsum("hqk,qhe->khe", low_probs, rows_grad, preferred_element_type=jnp.float32)
        )
        grad_probs = jnp.einsum(
            "qhe,khe->hqk", rows_grad, value_all[:last_row], preferred_element_type=jnp.float32
        )
        grad_scores = probs_full * (
            grad_probs - jnp.sum(probs_full * grad_probs, axis=-1, keepdims=True)
        )
        low_scores = grad_scores.astype(jnp.bfloat16)
        grad_query.append(
            jnp.einsum(
                "hqk,khe->qhe", low_scores, key_all[:last_row], preferred_element_type=jnp.float32
            )
            * score_scale
        )
        grad_key = grad_key.at[:last_row].add(
            jnp.einsum(
                "hqk,qhe->khe",
                low_scores,
                query_all[first_row:last_row],
                preferred_element_type=jnp.float32,
            )
            * score_scale
        )
    return (jnp.concatenate(grad_query, 0), grad_key, grad_value)


def body(
    hidden_in,
    ln1_gain,
    ln1_bias,
    qkv_weight,
    qv_bias,
    out_weight,
    out_bias,
    ln2_gain,
    ln2_bias,
    fc_weight,
    fc_bias,
    proj_weight,
    proj_bias,
    segment_ids,
    out_grad,
):
    width = hidden_in.shape[1]
    shard_pos = lax.axis_index("tensor")
    gathered = (
        lax.all_gather(ln1_gain, ("dp", "tensor"), axis=0, tiled=True),
        lax.all_gather(ln1_bias, ("dp", "tensor"), axis=0, tiled=True),
        lax.all_gather(qv_bias, ("dp", "tensor"), axis=0, tiled=True),
        lax.all_gather(out_bias, ("dp", "tensor"), axis=0, tiled=True),
        lax.all_gather(ln2_gain, ("dp", "tensor"), axis=0, tiled=True),
        lax.all_gather(ln2_bias, ("dp", "tensor"), axis=0, tiled=True),
        lax.all_gather(fc_bias, ("dp", "tensor"), axis=0, tiled=True),
        lax.all_gather(proj_bias, ("dp", "tensor"), axis=0, tiled=True),
    )
    gain_one, shift_one, qv_full, out_shift, gain_two, shift_two, fc_full, proj_shift = [
        vector.astype(jnp.float32) for vector in gathered
    ]
    qkv_local, out_local, fc_local, proj_local = (
        lax.all_gather(qkv_weight, "dp", axis=0, tiled=True),
        lax.all_gather(out_weight, "dp", axis=0, tiled=True),
        lax.all_gather(fc_weight, "dp", axis=0, tiled=True),
        lax.all_gather(proj_weight, "dp", axis=0, tiled=True),
    )
    head_cols = qkv_local.shape[2]
    heads_here = head_cols // HD
    ff_cols = fc_local.shape[1]
    ff_total = fc_full.shape[0]
    slopes_all = 2.0 ** (-8.0 * jnp.arange(1, HEADS + 1, dtype=jnp.float32) / HEADS)
    slopes = lax.dynamic_slice_in_dim(slopes_all, shard_pos * heads_here, heads_here)
    score_scale = HD ** (-0.5)
    q_shift = lax.dynamic_slice_in_dim(qv_full, shard_pos * head_cols, head_cols)
    v_shift = lax.dynamic_slice_in_dim(qv_full, width + shard_pos * head_cols, head_cols)
    source = hidden_in.astype(jnp.float32)
    normed_one = layer_norm(source, gain_one, shift_one)
    group_one = lax.all_gather(normed_one.astype(jnp.bfloat16), "tensor", axis=0, tiled=True)
    group_rows = group_one.shape[0]
    block_count = max(1, min(8, group_rows // 512))
    mixed = jnp.einsum("td,dcn->tcn", group_one, qkv_local, preferred_element_type=jnp.float32)
    queries = (mixed[:, 0] + q_shift).astype(jnp.bfloat16).reshape(group_rows, heads_here, HD)
    keys_here = mixed[:, 1].astype(jnp.bfloat16).reshape(group_rows, heads_here, HD)
    values_here = (mixed[:, 2] + v_shift).astype(jnp.bfloat16).reshape(group_rows, heads_here, HD)
    attended, log_sums = attend(
        queries, keys_here, values_here, segment_ids, slopes, score_scale, block_count
    )
    context = attended.reshape(group_rows, head_cols).astype(jnp.bfloat16)
    branch_one = lax.psum_scatter(
        contract_cols(context, out_local).astype(jnp.bfloat16),
        "tensor",
        scatter_dimension=0,
        tiled=True,
    ).astype(jnp.float32)
    middle = source + branch_one + out_shift
    normed_two = layer_norm(middle, gain_two, shift_two)
    low_two = normed_two.astype(jnp.bfloat16)
    group_two = lax.all_gather(low_two, "tensor", axis=0, tiled=True)
    fc_shift = lax.dynamic_slice_in_dim(fc_full, shard_pos * ff_cols, ff_cols)
    pre_act = jnp.dot(group_two, fc_local, preferred_element_type=jnp.float32) + fc_shift
    hidden_act = gelu_tanh(pre_act).astype(jnp.bfloat16)
    branch_two = (
        lax.psum_scatter(
            contract_cols(hidden_act, proj_local).astype(jnp.bfloat16),
            "tensor",
            scatter_dimension=0,
            tiled=True,
        ).astype(jnp.float32)
        + proj_shift
    )
    result = middle + branch_two
    group_top = lax.all_gather(out_grad, "tensor", axis=0, tiled=True)
    grad_hidden = jnp.dot(group_top, proj_local, preferred_element_type=jnp.float32)
    grad_proj_local = contract_rows(group_top, hidden_act)
    _, gelu_back = jax.vjp(gelu_tanh, pre_act)
    low_pre = gelu_back(grad_hidden)[0].astype(jnp.bfloat16)
    grad_fc_vec = lax.dynamic_update_slice_in_dim(
        jnp.zeros((ff_total,), jnp.float32),
        jnp.sum(low_pre.astype(jnp.float32), axis=0),
        shard_pos * ff_cols,
        0,
    )
    grad_fc_local = contract_rows(group_two, low_pre)
    grad_normed_two = lax.psum_scatter(
        contract_cols(low_pre, fc_local).astype(jnp.bfloat16),
        "tensor",
        scatter_dimension=0,
        tiled=True,
    ).astype(jnp.float32)
    grad_top = out_grad.astype(jnp.float32)
    grad_proj_vec = jnp.sum(grad_top, axis=0)
    _, norm_two_back = jax.vjp(layer_norm, middle, gain_two, shift_two)
    grad_middle_norm, grad_gain_two, grad_shift_two = norm_two_back(grad_normed_two)
    grad_middle = grad_top + grad_middle_norm
    low_mid = grad_middle.astype(jnp.bfloat16)
    grad_out_vec = jnp.sum(low_mid.astype(jnp.float32), axis=0)
    group_mid = lax.all_gather(low_mid, "tensor", axis=0, tiled=True)
    grad_context = jnp.dot(group_mid, out_local, preferred_element_type=jnp.float32)
    grad_out_local = contract_rows(group_mid, context)
    low_context = grad_context.astype(jnp.bfloat16).reshape(group_rows, heads_here, HD)
    grad_query, grad_key, grad_value = attend_back(
        queries,
        keys_here,
        values_here,
        segment_ids,
        slopes,
        score_scale,
        block_count,
        log_sums,
        low_context,
    )
    stacked = jnp.stack(
        [
            grad_query.reshape(group_rows, head_cols),
            grad_key.reshape(group_rows, head_cols),
            grad_value.reshape(group_rows, head_cols),
        ],
        axis=1,
    ).astype(jnp.bfloat16)
    grad_qkv_local = jnp.einsum(
        "td,tcn->dcn", group_one, stacked, preferred_element_type=jnp.float32
    )
    column_sums = jnp.sum(stacked.astype(jnp.float32), axis=0)
    grad_qv_vec = jnp.zeros((2 * width,), jnp.float32)
    grad_qv_vec = lax.dynamic_update_slice_in_dim(
        grad_qv_vec, column_sums[0], shard_pos * head_cols, 0
    )
    grad_qv_vec = lax.dynamic_update_slice_in_dim(
        grad_qv_vec, column_sums[2], width + shard_pos * head_cols, 0
    )
    grad_normed_one = lax.psum_scatter(
        jnp.einsum("tcn,dcn->td", stacked, qkv_local, preferred_element_type=jnp.float32).astype(
            jnp.bfloat16
        ),
        "tensor",
        scatter_dimension=0,
        tiled=True,
    ).astype(jnp.float32)
    _, norm_one_back = jax.vjp(layer_norm, source, gain_one, shift_one)
    grad_source_norm, grad_gain_one, grad_shift_one = norm_one_back(grad_normed_one)
    grad_input = grad_middle + grad_source_norm
    grad_qkv, grad_out_w, grad_fc_w, grad_proj_w = (
        lax.psum_scatter(
            grad_qkv_local.astype(jnp.bfloat16), "dp", scatter_dimension=0, tiled=True
        ).astype(jnp.float32),
        lax.psum_scatter(
            grad_out_local.astype(jnp.bfloat16), "dp", scatter_dimension=0, tiled=True
        ).astype(jnp.float32),
        lax.psum_scatter(
            grad_fc_local.astype(jnp.bfloat16), "dp", scatter_dimension=0, tiled=True
        ).astype(jnp.float32),
        lax.psum_scatter(
            grad_proj_local.astype(jnp.bfloat16), "dp", scatter_dimension=0, tiled=True
        ).astype(jnp.float32),
    )
    g_gain_one, g_shift_one, g_qv, g_out_b, g_gain_two, g_shift_two, g_fc_b, g_proj_b = (
        lax.psum_scatter(grad_gain_one, ("dp", "tensor"), scatter_dimension=0, tiled=True),
        lax.psum_scatter(grad_shift_one, ("dp", "tensor"), scatter_dimension=0, tiled=True),
        lax.psum_scatter(grad_qv_vec, ("dp", "tensor"), scatter_dimension=0, tiled=True),
        lax.psum_scatter(grad_out_vec, ("dp", "tensor"), scatter_dimension=0, tiled=True),
        lax.psum_scatter(grad_gain_two, ("dp", "tensor"), scatter_dimension=0, tiled=True),
        lax.psum_scatter(grad_shift_two, ("dp", "tensor"), scatter_dimension=0, tiled=True),
        lax.psum_scatter(grad_fc_vec, ("dp", "tensor"), scatter_dimension=0, tiled=True),
        lax.psum_scatter(grad_proj_vec, ("dp", "tensor"), scatter_dimension=0, tiled=True),
    )
    return (
        result.astype(jnp.bfloat16),
        grad_input.astype(jnp.bfloat16),
        g_gain_one,
        g_shift_one,
        grad_qkv,
        g_qv,
        grad_out_w,
        g_out_b,
        g_gain_two,
        g_shift_two,
        grad_fc_w,
        g_fc_b,
        grad_proj_w,
        g_proj_b,
    )


def solution(mesh):
    in_specs = (
        P(("dp", "tensor"), None),
        P(("dp", "tensor")),
        P(("dp", "tensor")),
        P("dp", None, "tensor"),
        P(("dp", "tensor")),
        P("dp", "tensor"),
        P(("dp", "tensor")),
        P(("dp", "tensor")),
        P(("dp", "tensor")),
        P("dp", "tensor"),
        P(("dp", "tensor")),
        P("dp", "tensor"),
        P(("dp", "tensor")),
        P("dp"),
        P(("dp", "tensor"), None),
    )
    out_specs = (
        P(("dp", "tensor"), None),
        P(("dp", "tensor"), None),
        P(("dp", "tensor")),
        P(("dp", "tensor")),
        P("dp", None, "tensor"),
        P(("dp", "tensor")),
        P("dp", "tensor"),
        P(("dp", "tensor")),
        P(("dp", "tensor")),
        P(("dp", "tensor")),
        P("dp", "tensor"),
        P(("dp", "tensor")),
        P("dp", "tensor"),
        P(("dp", "tensor")),
    )
    return jax.shard_map(body, mesh=mesh, in_specs=in_specs, out_specs=out_specs, check_vma=False)
```

profile of v0, /device:TPU:0, one launch (start us, length us, event | category | flops | bytes accessed | tf_op | source)
XLA Modules:
  0.0 894.8 jit_solution(17382423895905076569)
XLA Ops:
  15.0 43.3 %all-reduce.18 = (bf16[2048]{0:T(1024)(128)(2,1)S(1)}, bf16[1024]{0:T(1024)(128)(2,1)S(1)}, bf16[1024]{0:T(1024)(128)(2,1)S(1)}, bf16[1024]{0:T(1024)(128)(2,1)S...) all-reduce(bf16[2048]{0:T(1024)(128)(2,1)S(1)} %dynamic-update-slic, ...), channel_id=1, replica_groups=mesh['dp'=8,'tensor'=4] {'dp','tensor'}, use_global_device_ids=true, to_apply=%add.4 | all-reduce | flops 8192 | bytes 32768
  65.5 15.8 %all_gather.53 = bf16[1024,256]{1,0:T(8,128)(2,1)} all-gather(bf16[128,256]{1,0:T(8,128)(2,1)S(1)} %copy-done.64), channel_id=1, replica_groups=mesh['dp'=8,'tensor'=4] {'dp'}, dimensions={0}, use_global_device_ids=true | all-gather | bytes 589824 | tf_op jit(solution)/shard_map/all_gather | solution.py:162
  93.4 23.5 %all-gather.9.cloned.1.call-done = bf16[2048,1024]{1,0:T(8,128)(2,1)} async-done(((bf16[512,1024]{1,0:T(8,128)(2,1)}), bf16[2048,1024]{1,0:T(8,128)(2,1)}) %all-gather.9.cloned.1.call-update) | async-done | bytes 4194320 | tf_op jit(solution)/shard_map/all_gather | solution.py:177
  182.4 52.2 %reduce-scatter.11.cloned.1.call-done = bf16[512,1024]{1,0:T(8,128)(2,1)} async-done(((bf16[2048,1024]{1,0:T(8,128)(2,1)}), bf16[512,1024]{1,0:T(8,128)(2,1)}) %reduce-scatter.11.cloned.1.call-update) | async-done | bytes 1048592 | tf_op jit(solution)/shard_map/reduce_scatter | solution.py:188
  241.2 66.8 %all-gather = bf16[32,1,128]{2,1,0:T(2,128)(2,1)S(1)} all-gather(bf16[1,1,128]{2,1,0:T(2,128)(2,1)S(1)} %bitcast.211), channel_id=1, replica_groups=mesh['dp'=8,'tensor'=4] {'dp','tensor'}, dimensions={0}, use_global_device_ids=true | all-gather | bytes 8448 | tf_op jit(solution)/shard_map/all_gather | solution.py:154
  308.1 12.0 %all-gather.13.cloned.1.call-done = bf16[2048,1024]{1,0:T(8,128)(2,1)} async-done(((bf16[512,1024]{1,0:T(8,128)(2,1)}), bf16[2048,1024]{1,0:T(8,128)(2,1)}) %all-gather.13.cloned.1.call-update) | async-done | bytes 4194320 | tf_op jit(solution)/shard_map/all_gather | solution.py:197
  320.0 10.7 %fusion.136 = f32[2048,1024]{1,0:T(8,128)} fusion(bf16[2048,1024]{1,0:T(8,128)(2,1)} %all-gather.13.cloned.1.call-done, bf16[1024,1024]{1,0:T(8,128)(2,1)} %all-gather.15.cloned.1.call-done), kind=kOutput, calls=%fused_computation.202 | convolution fusion | flops 4294967296 | bytes 14680064 | tf_op jit(solution)/shard_map/dot_general | solution.py:199
  330.7 20.0 %all-gather.17.cloned.1.call-done = bf16[1024,1024]{1,0:T(8,128)(2,1)} async-done(((bf16[128,1024]{1,0:T(8,128)(2,1)}), bf16[1024,1024]{1,0:T(8,128)(2,1)}) %all-gather.17.cloned.1.call-update) | async-done | bytes 2097168 | tf_op jit(solution)/shard_map/all_gather | solution.py:164
  350.7 54.2 %all-gather.19.cloned.1.call-done = bf16[2048,1024]{1,0:T(8,128)(2,1)} async-done(((bf16[512,1024]{1,0:T(8,128)(2,1)}), bf16[2048,1024]{1,0:T(8,128)(2,1)}) %all-gather.19.cloned.1.call-update) | async-done | bytes 4194320 | tf_op jit(solution)/shard_map/all_gather | solution.py:211
  404.9 14.5 %convert_reduce_fusion = (f32[1024]{0:T(1024)}, bf16[2048,1024]{1,0:T(8,128)(2,1)S(1)}) fusion(f32[2048,1024]{1,0:T(8,128)} %fusion.136, f32[1024]{0:T(1024)S(1)} %dynamic_slice.15, bf16[2048,1024]{1,0:T(8,128)(2,1)} %all-gather.19.cloned.1.call-done, bf16[1024,1024]{1,0:T(8,128)(2,1)} %all-gather.17.cloned.1.call-done), kind=kOutput, calls=%fused_computation.27 | convolution fusion | flops 4343200768 | bytes 18882560 | tf_op jit(solution)/shard_map/dot_general | solution.py:212
  428.2 11.8 %convolution_convert_fusion.2 = bf16[2048,1024]{1,0:T(8,128)(2,1)} fusion(bf16[1024,1024]{1,0:T(8,128)(2,1)} %all-gather.17.cloned.1.call-done, f32[2048,1024]{1,0:T(8,128)} %fusion.136, f32[1024]{0:T(1024)S(1)} %dynamic_slice.15), kind=kOutput, calls=%fused_computation.61 | convolution fusion | flops 4318035968 | bytes 14684160 | tf_op jit(solution)/shard_map/dot_general | solution.py:31
  440.7 39.9 %reduce-scatter.15.cloned.1.call-done = bf16[512,1024]{1,0:T(8,128)(2,1)} async-done(((bf16[2048,1024]{1,0:T(8,128)(2,1)}), bf16[512,1024]{1,0:T(8,128)(2,1)}) %reduce-scatter.15.cloned.1.call-update) | async-done | bytes 1048592 | tf_op jit(solution)/shard_map/reduce_scatter | solution.py:223
  483.4 52.8 %reduce-scatter.13.cloned.1.call-done = bf16[512,1024]{1,0:T(8,128)(2,1)} async-done(((bf16[2048,1024]{1,0:T(8,128)(2,1)}), bf16[512,1024]{1,0:T(8,128)(2,1)}) %reduce-scatter.13.cloned.1.call-update) | async-done | bytes 1048592 | tf_op jit(solution)/shard_map/reduce_scatter | solution.py:202
  543.5 10.6 %convert_bitcast_fusion = bf16[1024,1024]{0,1:T(8,128)(2,1)S(1)} fusion(bf16[2048,1024]{1,0:T(8,128)(2,1)} %all-gather.19.cloned.1.call-done, f32[2048,1024]{1,0:T(8,128)} %fusion.136, f32[1024]{0:T(1024)S(1)} %dynamic_slice.15), kind=kOutput, calls=%fused_computation.119 | convolution fusion | flops 4316987392 | bytes 14684160 | tf_op jit(solution)/shard_map/dot_general | solution.py:25
  557.5 9.5 %convolution_convert_fusion.4 = bf16[1024,1024]{1,0:T(8,128)(2,1)} fusion(bf16[2048,1024]{1,0:T(8,128)(2,1)} %all-gather.13.cloned.1.call-done, bf16[2048,1024]{1,0:T(8,128)(2,1)} %copy-done.84), kind=kOutput, calls=%fused_computation.131 | convolution fusion | flops 4296015872 | bytes 10485760 | tf_op jit(solution)/shard_map/dot_general | solution.py:25
  567.1 29.0 %all-gather.21.cloned.1.call-done = bf16[2048,1024]{1,0:T(8,128)(2,1)} async-done(((bf16[512,1024]{1,0:T(8,128)(2,1)}), bf16[2048,1024]{1,0:T(8,128)(2,1)}) %all-gather.21.cloned.1.call-update) | async-done | bytes 4194320 | tf_op jit(solution)/shard_map/all_gather | solution.py:236
  616.7 11.1 %multiply_reduce_fusion.1 = (f32[4,512]{1,0:T(4,128)}, f32[4,512,1536]{2,1,0:T(8,128)}) fusion(f32[4,512,1536]{2,1,0:T(8,128)} %copy-done, f32[4,512]{1,0:T(4,128)S(1)} %log_add_fusion.1, bf16[512,4,64]{0,2,1:T(8,128)(2,1)S(1)} %bitcast.185, bf16[1536,4,64]{0,2,1:T(8,128)(2,1)S(1)} %bitcast.180), kind=kOutput, calls=%fused_computation.9 | convolution fusion | flops 412088320 | bytes 26230784 | tf_op jit(solution)/shard_map/qhe,khe->hqk/dot_general | solution.py:103
  627.9 9.1 %fusion.51 = f32[2048,4,64]{0,2,1:T(8,128)} fusion(f32[2048,4,64]{0,2,1:T(8,128)} %fusion.97, bf16[512,4,64]{0,2,1:T(8,128)(2,1)} %bitcast.186, f32[4,512,1536]{2,1,0:T(8,128)} %copy-done, f32[4,512]{1,0:T(4,128)S(1)} %log_add_fusion.1), kind=kOutput, calls=%fused_computation.93 | convolution fusion | flops 409337856 | bytes 15998976 | tf_op jit(solution)/shard_map/hqk,qhe->khe/dot_general | solution.py:101
  637.0 10.5 %multiply_reduce_fusion = (f32[4,512]{1,0:T(4,128)}, f32[4,512,2048]{2,1,0:T(8,128)}) fusion(f32[4,512,2048]{2,1,0:T(8,128)S(1)} %bitcast.161, f32[4,512]{1,0:T(4,128)} %log_add_fusion, bf16[512,4,64]{0,2,1:T(8,128)(2,1)} %bitcast.183, f32[2048,4,64]{0,2,1:T(8,128)} %bitcast.173, f32[4,64]{1,0:T(4,128)} %copy-done.79), kind=kOutput, calls=%fused_computation.1 | convolution fusion | flops 550500352 | bytes 35931136 | tf_op jit(solution)/shard_map/qhe,khe->hqk/dot_general | solution.py:103
  669.5 10.7 %multiply_convert_fusion.1 = bf16[4,512,1536]{2,1,0:T(8,128)(2,1)} fusion(f32[4,512,1536]{2,1,0:T(8,128)} %get-tuple-element.216, f32[4,512,1536]{2,1,0:T(8,128)S(1)} %bitcast.165, f32[4,512]{1,0:T(4,128)S(1)} %copy-done.66, f32[4,512]{1,0:T(4,128)S(1)} %log_add_fusion.1), kind=kLoop, calls=%fused_computation.8 | loop fusion | flops 12582912 | bytes 31473664 | tf_op jit(solution)/shard_map/convert_element_type | solution.py:109
  740.2 8.3 reduce-scatter.21.cloned.1.call-done
  750.0 33.2 %reduce-scatter.19.cloned.1.call-done = bf16[128,3,256]{2,0,1:T(8,128)(2,1)} async-done(((bf16[1024,3,256]{2,0,1:T(8,128)(2,1)}), bf16[128,3,256]{2,0,1:T(8,128)(2,1)}) %reduce-scatter.19.cloned.1.call-update) | async-done | bytes 196624 | tf_op jit(solution)/shard_map/reduce_scatter | solution.py:282
  784.9 51.7 %reduce-scatter.17.cloned.1.call-done = bf16[512,1024]{1,0:T(8,128)(2,1)} async-done(((bf16[2048,1024]{1,0:T(8,128)(2,1)}), bf16[512,1024]{1,0:T(8,128)(2,1)}) %reduce-scatter.17.cloned.1.call-update) | async-done | bytes 1048592 | tf_op jit(solution)/shard_map/reduce_scatter | solution.py:270
  843.2 40.1 %all-reduce.17 = (f32[1024]{0:T(1024)S(1)}, f32[1024]{0:T(1024)S(1)}, f32[2048]{0:T(1024)S(1)}, f32[1024]{0:T(1024)S(1)}, f32[1024]{0:T(1024)S(1)}, /*index=5*/f...) all-reduce(f32[1024]{0:T(1024)S(1)} %get-tuple-element.156, ...), channel_id=6, replica_groups=mesh['dp'=8,'tensor'=4] {'dp','tensor'}, use_global_device_ids=true, to_apply=%region_25.26.clone | all-reduce | flops 12288 | bytes 98304
  (377 shorter events, 238.1 us)
Async XLA Ops:
  7.2 58.3 %copy-start.61 = (s32[2048]{0:T(1024)S(1)}, s32[2048]{0:T(1024)}, u32[]{:S(2)}) copy-start(s32[2048]{0:T(1024)} %param.48) | copy-start | bytes 24580
  7.2 75.0 %slice-start.15 = ((s32[2048]{0:T(1024)}), s32[1024]{0:T(1024)S(1)}, s32[]{:S(2)}) async-start(s32[2048]{0:T(1024)} %param.48), calls=%async_computation.38 | async-start | bytes 8192 | tf_op jit(solution)/shard_map/slice | solution.py:61
  7.2 58.3 %copy-start.64 = (bf16[128,256]{1,0:T(8,128)(2,1)S(1)}, bf16[128,256]{1,0:T(8,128)(2,1)}, u32[]{:S(2)}) copy-start(bf16[128,256]{1,0:T(8,128)(2,1)} %param.40) | copy-start | bytes 196612
  7.2 86.2 %all-gather.11.cloned.1.call-start = ((), (), s32[]{:S(2)}) async-start(), calls=%async_computation.9 | async-start | bytes 1769472 | tf_op jit(solution)/shard_map/all_gather | solution.py:161
  9.0 107.9 %all-gather.9.cloned.1.call-start = ((), (), s32[]{:S(2)}) async-start(), calls=%async_computation.8 | async-start | bytes 5242880 | tf_op jit(solution)/shard_map/all_gather | solution.py:177
  64.0 170.6 %reduce-scatter.11.cloned.1.call-start = ((), (), s32[]{:S(2)}) async-start(), calls=%async_computation.10 | async-start | bytes 5242880 | tf_op jit(solution)/shard_map/reduce_scatter | solution.py:188
  64.2 105.2 %copy-start.79 = (f32[4,64]{1,0:T(4,128)}, f32[4,64]{1,0:T(4,128)S(1)}, u32[]{:S(2)}) copy-start(f32[4,64]{1,0:T(4,128)S(1)} %add.319) | copy-start | bytes 3076
  181.8 126.3 %all-gather.15.cloned.1.call-start = ((), (), s32[]{:S(2)}) async-start(), calls=%async_computation.12 | async-start | bytes 2359296 | tf_op jit(solution)/shard_map/all_gather | solution.py:163
  182.3 137.7 %all-gather.13.cloned.1.call-start = ((), (), s32[]{:S(2)}) async-start(), calls=%async_computation.11 | async-start | bytes 5242880 | tf_op jit(solution)/shard_map/all_gather | solution.py:197
  239.8 110.9 %all-gather.17.cloned.1.call-start = ((), (), s32[]{:S(2)}) async-start(), calls=%async_computation.13 | async-start | bytes 2359296 | tf_op jit(solution)/shard_map/all_gather | solution.py:164
  240.4 164.5 %all-gather.19.cloned.1.call-start = ((), (), s32[]{:S(2)}) async-start(), calls=%async_computation.15 | async-start | bytes 5242880 | tf_op jit(solution)/shard_map/all_gather | solution.py:211
  241.1 239.5 %reduce-scatter.15.cloned.1.call-start = ((), (), s32[]{:S(2)}) async-start(), calls=%async_computation.16 | async-start | bytes 5242880 | tf_op jit(solution)/shard_map/reduce_scatter | solution.py:223
  427.7 108.6 %reduce-scatter.13.cloned.1.call-start = ((), (), s32[]{:S(2)}) async-start(), calls=%async_computation.14 | async-start | bytes 5242880 | tf_op jit(solution)/shard_map/reduce_scatter | solution.py:202
  440.0 156.1 %all-gather.21.cloned.1.call-start = ((), (), s32[]{:S(2)}) async-start(), calls=%async_computation.17 | async-start | bytes 5242880 | tf_op jit(solution)/shard_map/all_gather | solution.py:236
  543.3 190.0 %reduce-scatter.25.cloned.1.call-start = ((), (), s32[]{:S(2)}) async-start(), calls=%async_computation.22 | async-start | bytes 2359296
  556.8 178.6 %reduce-scatter.23.cloned.1.call-start = ((), (), s32[]{:S(2)}) async-start(), calls=%async_computation.21 | async-start | bytes 2359296 | tf_op jit(solution)/shard_map/reduce_scatter | solution.py:288
  567.0 181.5 %reduce-scatter.21.cloned.1.call-start = ((), (), s32[]{:S(2)}) async-start(), calls=%async_computation.20 | async-start | bytes 589824 | tf_op jit(solution)/shard_map/reduce_scatter | solution.py:285
  717.5 65.7 %reduce-scatter.19.cloned.1.call-start = ((), (), s32[]{:S(2)}) async-start(), calls=%async_computation.19 | async-start | bytes 1769472 | tf_op jit(solution)/shard_map/reduce_scatter | solution.py:282
  725.2 111.4 %reduce-scatter.17.cloned.1.call-start = ((), (), s32[]{:S(2)}) async-start(), calls=%async_computation.18 | async-start | bytes 5242880 | tf_op jit(solution)/shard_map/reduce_scatter | solution.py:270
  732.4 104.1 %copy-start.60 = (f32[1024]{0:T(1024)S(1)}, f32[1024]{0:T(1024)}, u32[]{:S(2)}) copy-start(f32[1024]{0:T(1024)} %copy-done.59) | copy-start | bytes 12292
  732.4 104.1 %copy-start.63 = (f32[512]{0:T(512)S(1)}, f32[512]{0:T(512)}, u32[]{:S(2)}) copy-start(f32[512]{0:T(512)} %copy-done.62) | copy-start | bytes 6148
  732.5 106.2 %copy-start.75 = (f32[512]{0:T(512)S(1)}, f32[512]{0:T(512)}, u32[]{:S(2)}) copy-start(f32[512]{0:T(512)} %copy-done.74) | copy-start | bytes 6148
  732.5 106.2 %copy-start.72 = (f32[512]{0:T(512)S(1)}, f32[512]{0:T(512)}, u32[]{:S(2)}) copy-start(f32[512]{0:T(512)} %copy-done.71) | copy-start | bytes 6148
  737.2 104.0 %copy-start.10 = (f32[512,1024]{1,0:T(8,128)S(1)}, f32[512,1024]{1,0:T(8,128)}, u32[]{:S(2)}) copy-start(f32[512,1024]{1,0:T(8,128)} %copy-done.9) | copy-start | bytes 6291460
  (92 other events, 898.9 us)
Sparse Core Ops, SparseCore 0:
  10.2 30.2 all-gather.10
  64.1 52.7 all-gather.8
  181.9 52.6 reduce-scatter.10
  236.2 29.1 all-gather.14
  267.8 52.2 all-gather.12
  321.6 29.0 all-gather.16
  352.7 52.1 all-gather.18
  427.8 52.6 reduce-scatter.14
  483.5 52.6 reduce-scatter.12
  543.4 52.6 all-gather.20
  598.5 35.7 reduce-scatter.24
  636.6 34.4 reduce-scatter.22
  717.6 30.9 reduce-scatter.20
  750.7 32.4 reduce-scatter.18
  786.0 50.5 reduce-scatter.16
where the time goes:
time: 902 us; the launch traced here: 895 us
  waiting for transfers between devices  379 us (42%)
  matrix products  200 us (22%)
  blocking collectives  166 us (18%)
  other arithmetic  88 us (10%)
  local copies, waits for them, and re-layouts  45.4 us (5%)
  between operations  15.3 us (2%)
    unnamed x2, blocking collectives  83.4 us
    all_gather x1, blocking collectives, body(): lax.all_gather(fc_bias, ('dp', 'tensor'), axis=0, tiled=True)  66.8 us
    all_gather x1, waiting for transfers between devices, body(): group_top = lax.all_gather(out_grad, 'tensor', axis=0, tiled=True)  54.2 us
    reduce_scatter x1, waiting for transfers between devices, body(): lax.psum_scatter(contract_cols(hidden_act, proj_local).astype(jnp.bfloat1...  52.8 us
    reduce_scatter x1, waiting for transfers between devices, body(): lax.psum_scatter(contract_cols(context, out_local).astype(jnp.bfloat16),...  52.2 us
    reduce_scatter x1, waiting for transfers between devices, body(): lax.psum_scatter(jnp.einsum('tcn,dcn->td', stacked, qkv_local, preferred_...  51.7 us
    reduce_scatter x1, waiting for transfers between devices, body(): lax.psum_scatter(contract_cols(low_pre, fc_local).astype(jnp.bfloat16), '...  39.9 us
    reduce_scatter x1, waiting for transfers between devices, body(): lax.psum_scatter(grad_qkv_local.astype(jnp.bfloat16), 'dp', scatter_dimen...  33.2 us
  transfers between devices with their start and end apart: 15, of which 11 were waited for; matrix products, arithmetic and copies ran while one was open for 25% of the time, Pallas kernels for 0%

commit v1 on v0

v1 whole, which is shorter than its diff:
```python
import functools

import jax
import jax.numpy as jnp
from jax import lax
from jax.experimental import pallas as pl
from jax.experimental.pallas import tpu as pltpu
from jax.sharding import PartitionSpec as P

HEADS = 16
HD = 64


NEG_FILL = -1e30
EPSILON = 1e-05


def layer_norm(values, gain_vec, shift_vec):
    center = values - jnp.mean(values, axis=-1, keepdims=True)
    spread = jnp.mean(center * center, axis=-1, keepdims=True)
    return center * lax.rsqrt(spread + EPSILON) * gain_vec + shift_vec


def gelu_tanh(values):
    return jax.nn.gelu(values, approximate=True)


def contract_rows(left, right):
    return lax.dot_general(
        left, right, (((0,), (0,)), ((), ())), preferred_element_type=jnp.float32
    )


def contract_cols(left, right):
    return lax.dot_general(
        left, right, (((1,), (1,)), ((), ())), preferred_element_type=jnp.float32
    )


LOG2E = 1.4426950408889634
BLOCK = 512


def matmul(left, right):
    return jnp.dot(left, right, preferred_element_type=jnp.float32)


def mask_block(seg_col, seg_row, key_start, query_start, block):
    shape = (block, block)
    key_pos = key_start + lax.broadcasted_iota(jnp.int32, shape, 0)
    query_pos = query_start + lax.broadcasted_iota(jnp.int32, shape, 1)
    allowed = (seg_col == seg_row) & (key_pos <= query_pos)
    return jnp.where(allowed, 0.0, NEG_FILL)


def attend_kernel(
    heads, block, slope_ref, qt_ref, k_ref, vt_ref, segr_ref, segc_ref, ot_ref, lse_ref, kh, mask
):
    rows = k_ref.shape[0]
    for h in range(heads):
        kh[h] = k_ref[:, h * HD : (h + 1) * HD]
    scale = LOG2E * HD ** (-0.5)

    def query_loop(i, carry_none):
        q0 = pl.multiple_of(i * block, block)
        seg_row = segr_ref[:, pl.ds(q0, block)]

        def key_loop(j, state):
            k0 = pl.multiple_of(j * block, block)
            mask[...] = mask_block(segc_ref[pl.ds(k0, block), :], seg_row, k0, q0, block)
            pos = (k0 + lax.broadcasted_iota(jnp.int32, (block, 1), 0)).astype(jnp.float32)
            new_state = []
            for h in range(heads):
                top, total, acc = state[3 * h : 3 * h + 3]
                hs = slice(h * HD, (h + 1) * HD)
                raw = matmul(kh[h, pl.ds(k0, block), :], qt_ref[hs, pl.ds(q0, block)])
                score = raw * scale + (slope_ref[h] * pos + mask[...])
                new_top = jnp.maximum(top, jnp.max(score, axis=0, keepdims=True))
                prob = jnp.exp2(score - new_top)
                shrink = jnp.exp2(top - new_top)
                total = total * shrink + jnp.sum(prob, axis=0, keepdims=True)
                acc = acc * shrink + matmul(
                    vt_ref[hs, pl.ds(k0, block)], prob.astype(jnp.bfloat16)
                )
                new_state += [new_top, total, acc]
            return tuple(new_state)

        state = []
        for h in range(heads):
            state += [
                jnp.full((1, block), NEG_FILL, jnp.float32),
                jnp.zeros((1, block), jnp.float32),
                jnp.zeros((HD, block), jnp.float32),
            ]
        state = lax.fori_loop(0, i + 1, key_loop, tuple(state))
        for h in range(heads):
            top, total, acc = state[3 * h : 3 * h + 3]
            ot_ref[h * HD : (h + 1) * HD, pl.ds(q0, block)] = acc / total
            lse_ref[h, :, pl.ds(q0, block)] = top + jnp.log2(total)
        return carry_none

    lax.fori_loop(0, rows // block, query_loop, 0)


def attend_back_kernel(
    heads,
    block,
    slope_ref,
    q_ref,
    qt_ref,
    k_ref,
    kt_ref,
    v_ref,
    do_ref,
    dot_ref,
    ot_ref,
    lse_ref,
    segr_ref,
    segc_ref,
    dqt_ref,
    dk_ref,
    dv_ref,
    qh,
    kh,
    vh,
    doh,
    delta,
    dqt,
    mask,
):
    rows = k_ref.shape[0]
    for h in range(heads):
        hs = slice(h * HD, (h + 1) * HD)
        qh[h] = q_ref[:, hs]
        kh[h] = k_ref[:, hs]
        vh[h] = v_ref[:, hs]
        doh[h] = do_ref[:, hs]
        delta[h] = jnp.sum(dot_ref[hs, :].astype(jnp.float32) * ot_ref[hs, :], axis=0, keepdims=True)
    dqt[...] = jnp.zeros_like(dqt)
    scale = LOG2E * HD ** (-0.5)
    score_scale = HD ** (-0.5)
    count = rows // block

    def key_loop(j, carry_none):
        k0 = pl.multiple_of(j * block, block)
        pos = (k0 + lax.broadcasted_iota(jnp.int32, (block, 1), 0)).astype(jnp.float32)
        seg_col = segc_ref[pl.ds(k0, block), :]

        def query_loop(i, state):
            q0 = pl.multiple_of(i * block, block)
            mask[...] = mask_block(seg_col, segr_ref[:, pl.ds(q0, block)], k0, q0, block)
            new_state = []
            for h in range(heads):
                grad_k, grad_v = state[2 * h : 2 * h + 2]
                hs = slice(h * HD, (h + 1) * HD)
                raw = matmul(kh[h, pl.ds(k0, block), :], qt_ref[hs, pl.ds(q0, block)])
                score = raw * scale + (slope_ref[h] * pos + mask[...])
                prob = jnp.exp2(score - lse_ref[h, :, pl.ds(q0, block)])
                grad_p = matmul(vh[h, pl.ds(k0, block), :], dot_ref[hs, pl.ds(q0, block)])
                grad_s = (prob * (grad_p - delta[h, :, pl.ds(q0, block)])).astype(jnp.bfloat16)
                grad_v = grad_v + matmul(prob.astype(jnp.bfloat16), doh[h, pl.ds(q0, block), :])
                grad_k = grad_k + matmul(grad_s, qh[h, pl.ds(q0, block), :])
                dqt[hs, pl.ds(q0, block)] += matmul(kt_ref[hs, pl.ds(k0, block)], grad_s)
                new_state += [grad_k, grad_v]
            return tuple(new_state)

        zero = jnp.zeros((block, HD), jnp.float32)
        state = lax.fori_loop(j, count, query_loop, (zero,) * (2 * heads))
        for h in range(heads):
            hs = slice(h * HD, (h + 1) * HD)
            dk_ref[pl.ds(k0, block), hs] = (state[2 * h] * score_scale).astype(jnp.bfloat16)
            dv_ref[pl.ds(k0, block), hs] = state[2 * h + 1].astype(jnp.bfloat16)
        return carry_none

    lax.fori_loop(0, count, key_loop, 0)
    dqt_ref[...] = (dqt[...] * score_scale).astype(jnp.bfloat16)


def vmem_specs(count):
    return [pl.BlockSpec(memory_space=pltpu.SMEM)] + [
        pl.BlockSpec(memory_space=pltpu.VMEM) for _ in range(count)
    ]


def attend(queries_t, key_all, values_t, segments, slopes):
    rows, cols = key_all.shape
    heads = cols // HD
    block = min(BLOCK, rows)
    vm = pl.BlockSpec(memory_space=pltpu.VMEM)
    return pl.pallas_call(
        functools.partial(attend_kernel, heads, block),
        out_shape=(
            jax.ShapeDtypeStruct((cols, rows), jnp.float32),
            jax.ShapeDtypeStruct((heads, 1, rows), jnp.float32),
        ),
        in_specs=vmem_specs(5),
        out_specs=(vm, vm),
        scratch_shapes=[
            pltpu.VMEM((heads, rows, HD), jnp.bfloat16),
            pltpu.VMEM((block, block), jnp.float32),
        ],
        compiler_params=pltpu.CompilerParams(vmem_limit_bytes=48 * 2**20),
        cost_estimate=pl.CostEstimate(
            flops=40_000_000_000, bytes_accessed=8_000_000, transcendentals=0
        ),
    )(slopes * LOG2E, queries_t, key_all, values_t, segments[None, :], segments[:, None])


def attend_back(queries, queries_t, keys, values, segments, slopes, attended_t, log_sums, grad_out):
    rows, cols = keys.shape
    heads = cols // HD
    block = min(BLOCK, rows)
    vm = pl.BlockSpec(memory_space=pltpu.VMEM)
    per_head = pltpu.VMEM((heads, rows, HD), jnp.bfloat16)
    return pl.pallas_call(
        functools.partial(attend_back_kernel, heads, block),
        out_shape=(
            jax.ShapeDtypeStruct((cols, rows), jnp.bfloat16),
            jax.ShapeDtypeStruct((rows, cols), jnp.bfloat16),
            jax.ShapeDtypeStruct((rows, cols), jnp.bfloat16),
        ),
        in_specs=vmem_specs(11),
        out_specs=(vm, vm, vm),
        scratch_shapes=[
            per_head,
            per_head,
            per_head,
            per_head,
            pltpu.VMEM((heads, 1, rows), jnp.float32),
            pltpu.VMEM((cols, rows), jnp.float32),
            pltpu.VMEM((block, block), jnp.float32),
        ],
        compiler_params=pltpu.CompilerParams(vmem_limit_bytes=48 * 2**20),
        cost_estimate=pl.CostEstimate(
            flops=80_000_000_000, bytes_accessed=16_000_000, transcendentals=0
        ),
    )(
        slopes * LOG2E,
        queries,
        queries_t,
        keys,
        keys.T,
        values,
        grad_out,
        grad_out.T,
        attended_t,
        log_sums,
        segments[None, :],
        segments[:, None],
    )


def pad_lanes(values):
    return jnp.pad(values, ((0, 0), (0, -values.shape[1] % 128)))


def body(
    hidden_in,
    ln1_gain,
    ln1_bias,
    qkv_weight,
    qv_bias,
    out_weight,
    out_bias,
    ln2_gain,
    ln2_bias,
    fc_weight,
    fc_bias,
    proj_weight,
    proj_bias,
    segment_ids,
    out_grad,
):
    width = hidden_in.shape[1]
    shard_pos = lax.axis_index("tensor")
    small = (ln1_gain, ln1_bias, qv_bias, out_bias, ln2_gain, ln2_bias, fc_bias, proj_bias)
    packed = lax.all_gather(
        pad_lanes(jnp.concatenate(small)[None, :]), ("dp", "tensor"), axis=0, tiled=True
    ).astype(jnp.float32)
    device_count = packed.shape[0]
    vectors = []
    place = 0
    for vector in small:
        size = vector.shape[0]
        vectors.append(packed[:, place : place + size].reshape(device_count * size))
        place += size
    gain_one, shift_one, qv_full, out_shift, gain_two, shift_two, fc_full, proj_shift = vectors
    qkv_local, out_local, fc_local, proj_local = (
        lax.all_gather(qkv_weight, "dp", axis=0, tiled=True),
        lax.all_gather(out_weight, "dp", axis=0, tiled=True),
        lax.all_gather(fc_weight, "dp", axis=0, tiled=True),
        lax.all_gather(proj_weight, "dp", axis=0, tiled=True),
    )
    head_cols = qkv_local.shape[2]
    heads_here = head_cols // HD
    ff_cols = fc_local.shape[1]
    ff_total = fc_full.shape[0]
    slopes_all = 2.0 ** (-8.0 * jnp.arange(1, HEADS + 1, dtype=jnp.float32) / HEADS)
    slopes = lax.dynamic_slice_in_dim(slopes_all, shard_pos * heads_here, heads_here)
    q_shift = lax.dynamic_slice_in_dim(qv_full, shard_pos * head_cols, head_cols)
    v_shift = lax.dynamic_slice_in_dim(qv_full, width + shard_pos * head_cols, head_cols)
    source = hidden_in.astype(jnp.float32)
    normed_one = layer_norm(source, gain_one, shift_one)
    group_one = lax.all_gather(normed_one.astype(jnp.bfloat16), "tensor", axis=0, tiled=True)
    group_rows = group_one.shape[0]
    mixed = jnp.einsum("td,dcn->tcn", group_one, qkv_local, preferred_element_type=jnp.float32)
    queries = (mixed[:, 0] + q_shift).astype(jnp.bfloat16)
    keys_here = mixed[:, 1].astype(jnp.bfloat16)
    values_here = (mixed[:, 2] + v_shift).astype(jnp.bfloat16)
    queries_t = queries.T
    attended_t, log_sums = attend(queries_t, keys_here, values_here.T, segment_ids, slopes)
    context = attended_t.astype(jnp.bfloat16).T
    branch_one = lax.psum_scatter(
        contract_cols(context, out_local).astype(jnp.bfloat16),
        "tensor",
        scatter_dimension=0,
        tiled=True,
    ).astype(jnp.float32)
    middle = source + branch_one + out_shift
    normed_two = layer_norm(middle, gain_two, shift_two)
    low_two = normed_two.astype(jnp.bfloat16)
    group_two = lax.all_gather(low_two, "tensor", axis=0, tiled=True)
    fc_shift = lax.dynamic_slice_in_dim(fc_full, shard_pos * ff_cols, ff_cols)
    pre_act = jnp.dot(group_two, fc_local, preferred_element_type=jnp.float32) + fc_shift
    hidden_act = gelu_tanh(pre_act).astype(jnp.bfloat16)
    branch_two = (
        lax.psum_scatter(
            contract_cols(hidden_act, proj_local).astype(jnp.bfloat16),
            "tensor",
            scatter_dimension=0,
            tiled=True,
        ).astype(jnp.float32)
        + proj_shift
    )
    result = middle + branch_two
    group_top = lax.all_gather(out_grad, "tensor", axis=0, tiled=True)
    grad_hidden = jnp.dot(group_top, proj_local, preferred_element_type=jnp.float32)
    grad_proj_local = contract_rows(group_top, hidden_act)
    _, gelu_back = jax.vjp(gelu_tanh, pre_act)
    low_pre = gelu_back(grad_hidden)[0].astype(jnp.bfloat16)
    grad_fc_vec = lax.dynamic_update_slice_in_dim(
        jnp.zeros((ff_total,), jnp.float32),
        jnp.sum(low_pre.astype(jnp.float32), axis=0),
        shard_pos * ff_cols,
        0,
    )
    grad_fc_local = contract_rows(group_two, low_pre)
    grad_normed_two = lax.psum_scatter(
        contract_cols(low_pre, fc_local).astype(jnp.bfloat16),
        "tensor",
        scatter_dimension=0,
        tiled=True,
    ).astype(jnp.float32)
    grad_top = out_grad.astype(jnp.float32)
    grad_proj_vec = jnp.sum(grad_top, axis=0)
    _, norm_two_back = jax.vjp(layer_norm, middle, gain_two, shift_two)
    grad_middle_norm, grad_gain_two, grad_shift_two = norm_two_back(grad_normed_two)
    grad_middle = grad_top + grad_middle_norm
    low_mid = grad_middle.astype(jnp.bfloat16)
    grad_out_vec = jnp.sum(low_mid.astype(jnp.float32), axis=0)
    group_mid = lax.all_gather(low_mid, "tensor", axis=0, tiled=True)
    grad_context = jnp.dot(group_mid, out_local, preferred_element_type=jnp.float32)
    grad_out_local = contract_rows(group_mid, context)
    low_context = grad_context.astype(jnp.bfloat16)
    grad_query_t, grad_key, grad_value = attend_back(
        queries,
        queries_t,
        keys_here,
        values_here,
        segment_ids,
        slopes,
        attended_t,
        log_sums,
        low_context,
    )
    stacked = jnp.stack([grad_query_t.T, grad_key, grad_value], axis=1)
    grad_qkv_local = jnp.einsum(
        "td,tcn->dcn", group_one, stacked, preferred_element_type=jnp.float32
    )
    column_sums = jnp.sum(stacked.astype(jnp.float32), axis=0)
    grad_qv_vec = jnp.zeros((2 * width,), jnp.float32)
    grad_qv_vec = lax.dynamic_update_slice_in_dim(
        grad_qv_vec, column_sums[0], shard_pos * head_cols, 0
    )
    grad_qv_vec = lax.dynamic_update_slice_in_dim(
        grad_qv_vec, column_sums[2], width + shard_pos * head_cols, 0
    )
    grad_normed_one = lax.psum_scatter(
        jnp.einsum("tcn,dcn->td", stacked, qkv_local, preferred_element_type=jnp.float32).astype(
            jnp.bfloat16
        ),
        "tensor",
        scatter_dimension=0,
        tiled=True,
    ).astype(jnp.float32)
    _, norm_one_back = jax.vjp(layer_norm, source, gain_one, shift_one)
    grad_source_norm, grad_gain_one, grad_shift_one = norm_one_back(grad_normed_one)
    grad_input = grad_middle + grad_source_norm
    grad_qkv, grad_out_w, grad_fc_w, grad_proj_w = (
        lax.psum_scatter(
            grad_qkv_local.astype(jnp.bfloat16), "dp", scatter_dimension=0, tiled=True
        ).astype(jnp.float32),
        lax.psum_scatter(
            grad_out_local.astype(jnp.bfloat16), "dp", scatter_dimension=0, tiled=True
        ).astype(jnp.float32),
        lax.psum_scatter(
            grad_fc_local.astype(jnp.bfloat16), "dp", scatter_dimension=0, tiled=True
        ).astype(jnp.float32),
        lax.psum_scatter(
            grad_proj_local.astype(jnp.bfloat16), "dp", scatter_dimension=0, tiled=True
        ).astype(jnp.float32),
    )
    grads = (
        grad_gain_one,
        grad_shift_one,
        grad_qv_vec,
        grad_out_vec,
        grad_gain_two,
        grad_shift_two,
        grad_fc_vec,
        grad_proj_vec,
    )
    summed = lax.psum_scatter(
        pad_lanes(jnp.concatenate([vec.reshape(device_count, -1) for vec in grads], axis=1)),
        ("dp", "tensor"),
        scatter_dimension=0,
        tiled=True,
    ).reshape(-1)
    own = []
    place = 0
    for vector in small:
        size = vector.shape[0]
        own.append(summed[place : place + size])
        place += size
    g_gain_one, g_shift_one, g_qv, g_out_b, g_gain_two, g_shift_two, g_fc_b, g_proj_b = own
    return (
        result.astype(jnp.bfloat16),
        grad_input.astype(jnp.bfloat16),
        g_gain_one,
        g_shift_one,
        grad_qkv,
        g_qv,
        grad_out_w,
        g_out_b,
        g_gain_two,
        g_shift_two,
        grad_fc_w,
        g_fc_b,
        grad_proj_w,
        g_proj_b,
    )


def solution(mesh):
    in_specs = (
        P(("dp", "tensor"), None),
        P(("dp", "tensor")),
        P(("dp", "tensor")),
        P("dp", None, "tensor"),
        P(("dp", "tensor")),
        P("dp", "tensor"),
        P(("dp", "tensor")),
        P(("dp", "tensor")),
        P(("dp", "tensor")),
        P("dp", "tensor"),
        P(("dp", "tensor")),
        P("dp", "tensor"),
        P(("dp", "tensor")),
        P("dp"),
        P(("dp", "tensor"), None),
    )
    out_specs = (
        P(("dp", "tensor"), None),
        P(("dp", "tensor"), None),
        P(("dp", "tensor")),
        P(("dp", "tensor")),
        P("dp", None, "tensor"),
        P(("dp", "tensor")),
        P("dp", "tensor"),
        P(("dp", "tensor")),
        P(("dp", "tensor")),
        P(("dp", "tensor")),
        P("dp", "tensor"),
        P(("dp", "tensor")),
        P("dp", "tensor"),
        P(("dp", "tensor")),
    )
    return jax.shard_map(body, mesh=mesh, in_specs=in_specs, out_specs=out_specs, check_vma=False)
```

time: 902 us -> 856 us (0.949)
  matrix products: 200 us -> 95.5 us
  waiting for transfers between devices: 379 us -> 469 us
  Pallas kernels: 0 us -> 70.6 us
  other arithmetic: 88 us -> 34.9 us
  blocking collectives: 166 us -> 125 us
  local copies, waits for them, and re-layouts: 45.4 us -> 35.3 us
    dot_general x24 -> x0, matrix products: 104 us -> none  [the longest x4 27.8 us: attend_back(): jnp.einsum('qhe,khe->hqk', rows_grad, value_all[:last_row], preferred_ele...]
    pallas_call x0 -> x2, Pallas kernels: none -> 70.6 us  [the longest x1 44.8 us: attend_back(): pl.pallas_call(functools.partial(attend_back_kernel, heads, block), out_s...]
    unnamed x2 -> x1, blocking collectives: 83.4 us -> 39.8 us
    all_gather x1, waiting for transfers between devices: 12 us -> 54.6 us  [body(): group_two = lax.all_gather(low_two, 'tensor', axis=0, tiled=True)]
    convert_element_type x16 -> x2, other arithmetic: 34.2 us -> 3.87 us  [the longest x1 2.73 us: body(): values_here = (mixed[:, 2] + v_shift).astype(jnp.bfloat16)]
    all_gather x1, waiting for transfers between devices: 0.02 us -> 25 us  [body(): lax.all_gather(fc_weight, 'dp', axis=0, tiled=True)]
    reduce_scatter x1, waiting for transfers between devices: 8.35 us -> 26.9 us  [body(): lax.psum_scatter(grad_out_local.astype(jnp.bfloat16), 'dp', scatter_dimen...]
    unnamed x226 -> x75, local copies, waits for them, and re-layouts: 32.1 us -> 16.9 us
  transfers between devices with their start and end apart: 15 -> 15, of which waited for: 11 -> 12; matrix products, arithmetic and copies ran while one was open for 25% -> 12% of each run, Pallas kernels for 0% -> 5%
where the time goes in v1:
time: 856 us; the launch traced here: 847 us
  waiting for transfers between devices  469 us (55%)
  blocking collectives  125 us (15%)
  matrix products  95.5 us (11%)
  Pallas kernels  70.6 us (8%)
  local copies, waits for them, and re-layouts  35.3 us (4%)
  other arithmetic  34.9 us (4%)
  between operations  14.8 us (2%)
    all_gather x1, blocking collectives, body(): lax.all_gather(pad_lanes(jnp.concatenate(small)[None, :]), ('dp', 'tensor...  69.9 us
    all_gather x1, waiting for transfers between devices, body(): group_two = lax.all_gather(low_two, 'tensor', axis=0, tiled=True)  54.6 us
    all_gather x1, waiting for transfers between devices, body(): group_top = lax.all_gather(out_grad, 'tensor', axis=0, tiled=True)  54.2 us
    reduce_scatter x1, waiting for transfers between devices, body(): lax.psum_scatter(contract_cols(hidden_act, proj_local).astype(jnp.bfloat1...  53.4 us
    reduce_scatter x1, waiting for transfers between devices, body(): lax.psum_scatter(contract_cols(context, out_local).astype(jnp.bfloat16),...  52 us
    reduce_scatter x1, waiting for transfers between devices, body(): lax.psum_scatter(jnp.einsum('tcn,dcn->td', stacked, qkv_local, preferred_...  52 us
    pallas_call x1, Pallas kernels, attend_back(): pl.pallas_call(functools.partial(attend_back_kernel, heads, block), out_s...  44.8 us
    reduce_scatter x1, waiting for transfers between devices, body(): lax.psum_scatter(contract_cols(low_pre, fc_local).astype(jnp.bfloat16), '...  40.5 us
  transfers between devices with their start and end apart: 15, of which 12 were waited for; matrix products, arithmetic and copies ran while one was open for 12% of the time, Pallas kernels for 5%

profile of v1, /device:TPU:0, one launch (start us, length us, event | category | flops | bytes accessed | tf_op | source)
XLA Modules:
  0.0 847.0 jit_solution(9566020647807228182)
XLA Ops:
  13.4 69.9 %all-gather.1 = bf16[32,1,384]{2,1,0:T(2,128)(2,1)S(1)} all-gather(bf16[1,1,384]{2,1,0:T(2,128)(2,1)S(1)} %reshape.153), channel_id=2, replica_groups=mesh['dp'=8,'tensor'=4] {'dp','tensor'}, dimensions={0}, use_global_device_ids=true | all-gather | bytes 25344 | tf_op jit(solution)/shard_map/all_gather | solution.py:277
  87.7 15.8 %all_gather.30 = bf16[1024,256]{1,0:T(8,128)(2,1)} all-gather(bf16[128,256]{1,0:T(8,128)(2,1)S(1)} %copy-done.26), channel_id=1, replica_groups=mesh['dp'=8,'tensor'=4] {'dp'}, dimensions={0}, use_global_device_ids=true | all-gather | bytes 589824 | tf_op jit(solution)/shard_map/all_gather | solution.py:290
  103.6 32.1 %all-gather.10.cloned.1.call-done = bf16[2048,1024]{1,0:T(8,128)(2,1)} async-done(((bf16[512,1024]{1,0:T(8,128)(2,1)}), bf16[2048,1024]{1,0:T(8,128)(2,1)}) %all-gather.10.cloned.1.call-update) | async-done | bytes 4194320 | tf_op jit(solution)/shard_map/all_gather | solution.py:304
  153.2 25.7 %shard_map.254 = (f32[256,2048]{1,0:T(8,128)}, f32[4,1,2048]{2,1,0:T(1,128)S(1)}) custom-call(f32[4]{0:T(128)S(1)} %dynamic-slice_multiply_fusion.slope_ref, bf16[256,2048]{1,0:T(8,128)(2,1)S(1)} %fusion.65.qt_ref, bf16[2048,256]{1,0:T(8,128)(2,1)S(1)} %copy.55.k_ref, bf16[256,2048]{1,0:T(8,128)(2,1)S(1)} %copy-done.4, s32[1,2048]{1,0:T(1,128)S(1)} %bitcast.93, ...), custom_call_target="tpu_custom_call" | custom-call | flops 40000000000 | bytes 8000000 | tf_op jit(solution)/shard_map/pallas_call | solution.py:190
  184.6 52.0 %reduce-scatter.11.cloned.1.call-done = bf16[512,1024]{1,0:T(8,128)(2,1)} async-done(((bf16[2048,1024]{1,0:T(8,128)(2,1)}), bf16[512,1024]{1,0:T(8,128)(2,1)}) %reduce-scatter.11.cloned.1.call-update) | async-done | bytes 1048592 | tf_op jit(solution)/shard_map/reduce_scatter | solution.py:313
  242.3 25.0 %all-gather.16.cloned.1.call-done = bf16[1024,1024]{1,0:T(8,128)(2,1)} async-done(((bf16[128,1024]{1,0:T(8,128)(2,1)}), bf16[1024,1024]{1,0:T(8,128)(2,1)}) %all-gather.16.cloned.1.call-update) | async-done | bytes 2097168 | tf_op jit(solution)/shard_map/all_gather | solution.py:291
  267.3 54.6 %all-gather.14.cloned.1.call-done = bf16[2048,1024]{1,0:T(8,128)(2,1)} async-done(((bf16[512,1024]{1,0:T(8,128)(2,1)}), bf16[2048,1024]{1,0:T(8,128)(2,1)}) %all-gather.14.cloned.1.call-update) | async-done | bytes 4194320 | tf_op jit(solution)/shard_map/all_gather | solution.py:322
  321.9 10.6 %fusion.47 = f32[2048,1024]{1,0:T(8,128)} fusion(bf16[2048,1024]{1,0:T(8,128)(2,1)} %all-gather.14.cloned.1.call-done, bf16[1024,1024]{1,0:T(8,128)(2,1)} %all-gather.16.cloned.1.call-done), kind=kOutput, calls=%fused_computation.99 | convolution fusion | flops 4294967296 | bytes 14680064 | tf_op jit(solution)/shard_map/dot_general | solution.py:324
  332.6 20.1 %all-gather.18.cloned.1.call-done = bf16[1024,1024]{1,0:T(8,128)(2,1)} async-done(((bf16[128,1024]{1,0:T(8,128)(2,1)}), bf16[1024,1024]{1,0:T(8,128)(2,1)}) %all-gather.18.cloned.1.call-update) | async-done | bytes 2097168 | tf_op jit(solution)/shard_map/all_gather | solution.py:292
  352.6 54.2 %all-gather.20.cloned.1.call-done = bf16[2048,1024]{1,0:T(8,128)(2,1)} async-done(((bf16[512,1024]{1,0:T(8,128)(2,1)}), bf16[2048,1024]{1,0:T(8,128)(2,1)}) %all-gather.20.cloned.1.call-update) | async-done | bytes 4194320 | tf_op jit(solution)/shard_map/all_gather | solution.py:336
  406.8 14.3 %convert_reduce_fusion = (f32[1024]{0:T(1024)}, bf16[2048,1024]{1,0:T(8,128)(2,1)S(1)}) fusion(f32[2048,1024]{1,0:T(8,128)} %fusion.47, f32[1024]{0:T(1024)S(1)} %dynamic_slice.15, bf16[2048,1024]{1,0:T(8,128)(2,1)} %all-gather.20.cloned.1.call-done, bf16[1024,1024]{1,0:T(8,128)(2,1)} %all-gather.18.cloned.1.call-done), kind=kOutput, calls=%fused_computation.10 | convolution fusion | flops 4343200768 | bytes 18882560 | tf_op jit(solution)/shard_map/dot_general | solution.py:337
  429.8 11.7 %convolution_convert_fusion.2 = bf16[2048,1024]{1,0:T(8,128)(2,1)} fusion(bf16[1024,1024]{1,0:T(8,128)(2,1)} %all-gather.18.cloned.1.call-done, f32[2048,1024]{1,0:T(8,128)} %fusion.47, f32[1024]{0:T(1024)S(1)} %dynamic_slice.15), kind=kOutput, calls=%fused_computation.19 | convolution fusion | flops 4318035968 | bytes 14684160 | tf_op jit(solution)/shard_map/dot_general | solution.py:35
  441.7 40.5 %reduce-scatter.15.cloned.1.call-done = bf16[512,1024]{1,0:T(8,128)(2,1)} async-done(((bf16[2048,1024]{1,0:T(8,128)(2,1)}), bf16[512,1024]{1,0:T(8,128)(2,1)}) %reduce-scatter.15.cloned.1.call-update) | async-done | bytes 1048592 | tf_op jit(solution)/shard_map/reduce_scatter | solution.py:348
  484.6 53.4 %reduce-scatter.13.cloned.1.call-done = bf16[512,1024]{1,0:T(8,128)(2,1)} async-done(((bf16[2048,1024]{1,0:T(8,128)(2,1)}), bf16[512,1024]{1,0:T(8,128)(2,1)}) %reduce-scatter.13.cloned.1.call-update) | async-done | bytes 1048592 | tf_op jit(solution)/shard_map/reduce_scatter | solution.py:327
  543.8 10.6 %convert_bitcast_fusion = bf16[1024,1024]{0,1:T(8,128)(2,1)S(1)} fusion(bf16[2048,1024]{1,0:T(8,128)(2,1)} %all-gather.20.cloned.1.call-done, f32[2048,1024]{1,0:T(8,128)} %fusion.47, f32[1024]{0:T(1024)S(1)} %dynamic_slice.15), kind=kOutput, calls=%fused_computation.56 | convolution fusion | flops 4316987392 | bytes 14684160 | tf_op jit(solution)/shard_map/dot_general | solution.py:29
  564.6 9.3 %convolution_convert_fusion.4 = bf16[1024,1024]{1,0:T(8,128)(2,1)} fusion(bf16[2048,1024]{1,0:T(8,128)(2,1)} %all-gather.14.cloned.1.call-done, bf16[2048,1024]{1,0:T(8,128)(2,1)} %copy-done.33), kind=kOutput, calls=%fused_computation.62 | convolution fusion | flops 4296015872 | bytes 10485760 | tf_op jit(solution)/shard_map/dot_general | solution.py:29
  574.3 22.1 %all-gather.22.cloned.1.call-done = bf16[2048,1024]{1,0:T(8,128)(2,1)} async-done(((bf16[512,1024]{1,0:T(8,128)(2,1)}), bf16[2048,1024]{1,0:T(8,128)(2,1)}) %all-gather.22.cloned.1.call-update) | async-done | bytes 4194320 | tf_op jit(solution)/shard_map/all_gather | solution.py:361
  602.4 44.8 %shard_map.255 = (bf16[256,2048]{1,0:T(8,128)(2,1)S(1)}, bf16[2048,256]{1,0:T(8,128)(2,1)S(1)}, bf16[2048,256]{1,0:T(8,128)(2,1)S(1)}) custom-call(f32[4]{0:T(128)S(1)} %dynamic-slice_multiply_fusion.slope_ref, bf16[2048,256]{1,0:T(8,128)(2,1)S(1)} %copy-done.2, bf16[256,2048]{1,0:T(8,128)(2,1)S(1)} %fusion.65.qt_ref, bf16[2048,256]{1,0:T(8,128)(2,1)} %copy-done.1, ...), custom_call_target="tpu_custom_call" | custom-call | flops 80000000000 | bytes 16000000 | tf_op jit(solution)/shard_map/pallas_call | solution.py:215
  655.5 6.9 fusion.30
  662.5 6.4 bitcast_convert_fusion
  676.3 26.9 %reduce-scatter.21.cloned.1.call-done = bf16[128,256]{1,0:T(8,128)(2,1)} async-done(((bf16[1024,256]{1,0:T(8,128)(2,1)}), bf16[128,256]{1,0:T(8,128)(2,1)}) %reduce-scatter.21.cloned.1.call-update) | async-done | bytes 65552 | tf_op jit(solution)/shard_map/reduce_scatter | solution.py:403
  704.8 33.1 %reduce-scatter.19.cloned.1.call-done = bf16[128,3,256]{2,0,1:T(8,128)(2,1)} async-done(((bf16[1024,3,256]{2,0,1:T(8,128)(2,1)}), bf16[128,3,256]{2,0,1:T(8,128)(2,1)}) %reduce-scatter.19.cloned.1.call-update) | async-done | bytes 196624 | tf_op jit(solution)/shard_map/reduce_scatter | solution.py:400
  739.5 52.0 %reduce-scatter.17.cloned.1.call-done = bf16[512,1024]{1,0:T(8,128)(2,1)} async-done(((bf16[2048,1024]{1,0:T(8,128)(2,1)}), bf16[512,1024]{1,0:T(8,128)(2,1)}) %reduce-scatter.17.cloned.1.call-update) | async-done | bytes 1048592 | tf_op jit(solution)/shard_map/reduce_scatter | solution.py:388
  798.5 39.8 %all-reduce = f32[32,384]{1,0:T(8,128)S(1)} all-reduce(f32[32,384]{1,0:T(8,128)S(1)} %concatenate.7), channel_id=7, replica_groups=mesh['dp'=8,'tensor'=4] {'dp','tensor'}, use_global_device_ids=true, to_apply=%region_20.21.clone | all-reduce | flops 12288 | bytes 98304
  (181 shorter events, 100.2 us)
Async XLA Ops:
  7.2 77.8 %copy-start.6 = (bf16[512,1024]{1,0:T(8,128)(2,1)S(1)}, bf16[512,1024]{1,0:T(8,128)(2,1)}, u32[]{:S(2)}) copy-start(bf16[512,1024]{1,0:T(8,128)(2,1)} %param.15) | copy-start | bytes 3145732
  7.2 96.4 %all-gather.12.cloned.1.call-start = ((), (), s32[]{:S(2)}) async-start(), calls=%async_computation.9 | async-start | bytes 1769472 | tf_op jit(solution)/shard_map/all_gather | solution.py:289
  7.9 127.7 %all-gather.10.cloned.1.call-start = ((), (), s32[]{:S(2)}) async-start(), calls=%async_computation.8 | async-start | bytes 5242880 | tf_op jit(solution)/shard_map/all_gather | solution.py:304
  87.0 149.7 %reduce-scatter.11.cloned.1.call-start = ((), (), s32[]{:S(2)}) async-start(), calls=%async_computation.10 | async-start | bytes 5242880 | tf_op jit(solution)/shard_map/reduce_scatter | solution.py:313
  87.5 65.6 %copy-start = (s32[2048,1]{1,0:T(8,128)}, s32[2048,1]{1,0:T(8,128)S(1)}, u32[]{:S(2)}) copy-start(s32[2048,1]{1,0:T(8,128)S(1)} %copy.57.segc_ref) | copy-start | bytes 24580
  183.8 52.9 %copy-start.7 = (bf16[512,1024]{1,0:T(8,128)(2,1)S(1)}, bf16[512,1024]{1,0:T(8,128)(2,1)}, u32[]{:S(2)}) copy-start(bf16[512,1024]{1,0:T(8,128)(2,1)} %param.15) | copy-start | bytes 3145732
  183.8 83.5 %all-gather.16.cloned.1.call-start = ((), (), s32[]{:S(2)}) async-start(), calls=%async_computation.12 | async-start | bytes 2359296 | tf_op jit(solution)/shard_map/all_gather | solution.py:291
  184.4 137.6 %all-gather.14.cloned.1.call-start = ((), (), s32[]{:S(2)}) async-start(), calls=%async_computation.11 | async-start | bytes 5242880 | tf_op jit(solution)/shard_map/all_gather | solution.py:322
  240.6 112.0 %all-gather.18.cloned.1.call-start = ((), (), s32[]{:S(2)}) async-start(), calls=%async_computation.13 | async-start | bytes 2359296 | tf_op jit(solution)/shard_map/all_gather | solution.py:292
  241.2 165.7 %all-gather.20.cloned.1.call-start = ((), (), s32[]{:S(2)}) async-start(), calls=%async_computation.15 | async-start | bytes 5242880 | tf_op jit(solution)/shard_map/all_gather | solution.py:336
  241.9 240.3 %reduce-scatter.15.cloned.1.call-start = ((), (), s32[]{:S(2)}) async-start(), calls=%async_computation.16 | async-start | bytes 5242880 | tf_op jit(solution)/shard_map/reduce_scatter | solution.py:348
  429.4 108.6 %reduce-scatter.13.cloned.1.call-start = ((), (), s32[]{:S(2)}) async-start(), calls=%async_computation.14 | async-start | bytes 5242880 | tf_op jit(solution)/shard_map/reduce_scatter | solution.py:327
  441.6 154.8 %all-gather.22.cloned.1.call-start = ((), (), s32[]{:S(2)}) async-start(), calls=%async_computation.17 | async-start | bytes 5242880 | tf_op jit(solution)/shard_map/all_gather | solution.py:361
  543.5 126.3 %reduce-scatter.25.cloned.1.call-start = ((), (), s32[]{:S(2)}) async-start(), calls=%async_computation.22 | async-start | bytes 2359296
  556.9 115.0 %reduce-scatter.23.cloned.1.call-start = ((), (), s32[]{:S(2)}) async-start(), calls=%async_computation.21 | async-start | bytes 2359296 | tf_op jit(solution)/shard_map/reduce_scatter | solution.py:406
  574.0 129.2 %reduce-scatter.21.cloned.1.call-start = ((), (), s32[]{:S(2)}) async-start(), calls=%async_computation.20 | async-start | bytes 589824 | tf_op jit(solution)/shard_map/reduce_scatter | solution.py:403
  655.2 82.6 %reduce-scatter.19.cloned.1.call-start = ((), (), s32[]{:S(2)}) async-start(), calls=%async_computation.19 | async-start | bytes 1769472 | tf_op jit(solution)/shard_map/reduce_scatter | solution.py:400
  662.5 129.0 %reduce-scatter.17.cloned.1.call-start = ((), (), s32[]{:S(2)}) async-start(), calls=%async_computation.18 | async-start | bytes 5242880 | tf_op jit(solution)/shard_map/reduce_scatter | solution.py:388
  673.7 117.8 %copy-start.8 = (bf16[512,1024]{1,0:T(8,128)(2,1)S(1)}, bf16[512,1024]{1,0:T(8,128)(2,1)}, u32[]{:S(2)}) copy-start(bf16[512,1024]{1,0:T(8,128)(2,1)} %param.15) | copy-start | bytes 3145732
  673.7 117.8 %copy-start.23 = (f32[1024]{0:T(1024)S(1)}, f32[1024]{0:T(1024)}, u32[]{:S(2)}) copy-start(f32[1024]{0:T(1024)} %copy-done.22) | copy-start | bytes 12292
  673.7 117.8 %copy-start.25 = (f32[512]{0:T(512)S(1)}, f32[512]{0:T(512)}, u32[]{:S(2)}) copy-start(f32[512]{0:T(512)} %copy-done.24) | copy-start | bytes 6148
  675.7 117.8 %copy-start.30 = (f32[512]{0:T(512)S(1)}, f32[512]{0:T(512)}, u32[]{:S(2)}) copy-start(f32[512]{0:T(512)} %copy-done.29) | copy-start | bytes 6148
  675.7 117.9 %copy-start.28 = (f32[512]{0:T(512)S(1)}, f32[512]{0:T(512)}, u32[]{:S(2)}) copy-start(f32[512]{0:T(512)} %copy-done.27) | copy-start | bytes 6148
  739.5 56.5 %copy-start.11 = (f32[512,1024]{1,0:T(8,128)S(1)}, f32[512,1024]{1,0:T(8,128)}, u32[]{:S(2)}) copy-start(f32[512,1024]{1,0:T(8,128)} %copy-done.10) | copy-start | bytes 6291460
  (25 other events, 150.0 us)
Sparse Core Ops, SparseCore 0:
  9.6 27.7 all-gather.11
  87.1 48.5 all-gather.9
  183.9 52.6 reduce-scatter.10
  238.2 29.0 all-gather.15
  269.7 52.1 all-gather.13
  323.5 29.0 all-gather.17
  354.6 52.1 all-gather.19
  429.5 52.6 reduce-scatter.14
  485.2 52.6 reduce-scatter.12
  543.7 52.6 all-gather.21
  598.8 35.7 reduce-scatter.24
  636.9 34.4 reduce-scatter.22
  673.7 29.5 reduce-scatter.20
  705.4 32.3 reduce-scatter.18
  740.6 50.8 reduce-scatter.16

commit v2 on v1

--- a/solution.py
+++ b/solution.py
@@ -254,6 +254,69 @@
     return jnp.pad(values, ((0, 0), (0, -values.shape[1] % 128)))
 
 
+def swap_pairs(count, unit, step):
+    return [(j, (((j // unit) ^ step) * unit) + j % unit) for j in range(count)]
+
+
+def place_at(buffer, part, index):
+    return lax.dynamic_update_slice_in_dim(buffer, part[None], index, 0)
+
+
+def gather_level(values, axis, unit):
+    count = lax.axis_size(axis)
+    group = lax.axis_index(axis) // unit
+    buffer = place_at(jnp.zeros((count // unit,) + values.shape, values.dtype), values, group)
+    for step in range(1, count // unit):
+        part = lax.ppermute(values, axis, swap_pairs(count, unit, step))
+        buffer = place_at(buffer, part, group ^ step)
+    return buffer
+
+
+def gather_tensor(values):
+    buffer = gather_level(values, "tensor", 1)
+    return buffer.reshape((-1,) + values.shape[1:])
+
+
+def gather_dp(values):
+    count = lax.axis_size("dp")
+    core = lax.axis_index("dp") % 2
+    mine = gather_level(values, "dp", 2)
+    other = lax.ppermute(mine, "dp", [(j, j ^ 1) for j in range(count)])
+    first = jnp.where(core == 0, mine, other)
+    second = jnp.where(core == 0, other, mine)
+    return jnp.stack([first, second], axis=1).reshape((-1,) + values.shape[1:])
+
+
+def pick(values, index):
+    return lax.dynamic_index_in_dim(values, index, 0, keepdims=False)
+
+
+def reduce_level(values, axis, unit):
+    count = lax.axis_size(axis)
+    group = lax.axis_index(axis) // unit
+    total = pick(values, group).astype(jnp.float32)
+    for step in range(1, count // unit):
+        part = lax.ppermute(pick(values, group ^ step), axis, swap_pairs(count, unit, step))
+        total = total + part.astype(jnp.float32)
+    return total
+
+
+def reduce_tensor(values):
+    parts = lax.axis_size("tensor")
+    return reduce_level(values.reshape((parts, -1) + values.shape[1:]), "tensor", 1)
+
+
+def reduce_dp(values):
+    count = lax.axis_size("dp")
+    core = lax.axis_index("dp") % 2
+    split = values.reshape((count // 2, 2, values.shape[0] // count) + values.shape[1:])
+    keep = lax.dynamic_index_in_dim(split, core, 1, keepdims=False)
+    send = lax.dynamic_index_in_dim(split, 1 - core, 1, keepdims=False)
+    came = lax.ppermute(send, "dp", [(j, j ^ 1) for j in range(count)])
+    both = keep.astype(jnp.float32) + came.astype(jnp.float32)
+    return reduce_level(both.astype(values.dtype), "dp", 2)
+
+
 def body(
     hidden_in,
     ln1_gain,
@@ -274,9 +337,9 @@
     width = hidden_in.shape[1]
     shard_pos = lax.axis_index("tensor")
     small = (ln1_gain, ln1_bias, qv_bias, out_bias, ln2_gain, ln2_bias, fc_bias, proj_bias)
-    packed = lax.all_gather(
-        pad_lanes(jnp.concatenate(small)[None, :]), ("dp", "tensor"), axis=0, tiled=True
-    ).astype(jnp.float32)
+    packed = gather_dp(gather_tensor(pad_lanes(jnp.concatenate(small)[None, :]))).astype(
+        jnp.float32
+    )
     device_count = packed.shape[0]
     vectors = []
     place = 0
@@ -287,9 +350,9 @@
     gain_one, shift_one, qv_full, out_shift, gain_two, shift_two, fc_full, proj_shift = vectors
     qkv_local, out_local, fc_local, proj_local = (
         lax.all_gather(qkv_weight, "dp", axis=0, tiled=True),
-        lax.all_gather(out_weight, "dp", axis=0, tiled=True),
-        lax.all_gather(fc_weight, "dp", axis=0, tiled=True),
-        lax.all_gather(proj_weight, "dp", axis=0, tiled=True),
+        gather_dp(out_weight),
+        gather_dp(fc_weight),
+        gather_dp(proj_weight),
     )
     head_cols = qkv_local.shape[2]
     heads_here = head_cols // HD
@@ -324,16 +387,10 @@
     pre_act = jnp.dot(group_two, fc_local, preferred_element_type=jnp.float32) + fc_shift
     hidden_act = gelu_tanh(pre_act).astype(jnp.bfloat16)
     branch_two = (
-        lax.psum_scatter(
-            contract_cols(hidden_act, proj_local).astype(jnp.bfloat16),
-            "tensor",
-            scatter_dimension=0,
-            tiled=True,
-        ).astype(jnp.float32)
-        + proj_shift
+        reduce_tensor(contract_cols(hidden_act, proj_local).astype(jnp.bfloat16)) + proj_shift
     )
     result = middle + branch_two
-    group_top = lax.all_gather(out_grad, "tensor", axis=0, tiled=True)
+    group_top = gather_tensor(out_grad)
     grad_hidden = jnp.dot(group_top, proj_local, preferred_element_type=jnp.float32)
     grad_proj_local = contract_rows(group_top, hidden_act)
     _, gelu_back = jax.vjp(gelu_tanh, pre_act)
@@ -397,18 +454,10 @@
     grad_source_norm, grad_gain_one, grad_shift_one = norm_one_back(grad_normed_one)
     grad_input = grad_middle + grad_source_norm
     grad_qkv, grad_out_w, grad_fc_w, grad_proj_w = (
-        lax.psum_scatter(
-            grad_qkv_local.astype(jnp.bfloat16), "dp", scatter_dimension=0, tiled=True
-        ).astype(jnp.float32),
-        lax.psum_scatter(
-            grad_out_local.astype(jnp.bfloat16), "dp", scatter_dimension=0, tiled=True
-        ).astype(jnp.float32),
-        lax.psum_scatter(
-            grad_fc_local.astype(jnp.bfloat16), "dp", scatter_dimension=0, tiled=True
-        ).astype(jnp.float32),
-        lax.psum_scatter(
-            grad_proj_local.astype(jnp.bfloat16), "dp", scatter_dimension=0, tiled=True
-        ).astype(jnp.float32),
+        reduce_dp(grad_qkv_local.astype(jnp.bfloat16)),
+        reduce_dp(grad_out_local.astype(jnp.bfloat16)),
+        reduce_dp(grad_fc_local.astype(jnp.bfloat16)),
+        reduce_dp(grad_proj_local.astype(jnp.bfloat16)),
     )
     grads = (
         grad_gain_one,
@@ -420,12 +469,10 @@
         grad_fc_vec,
         grad_proj_vec,
     )
-    summed = lax.psum_scatter(
-        pad_lanes(jnp.concatenate([vec.reshape(device_count, -1) for vec in grads], axis=1)),
-        ("dp", "tensor"),
-        scatter_dimension=0,
-        tiled=True,
-    ).reshape(-1)
+    table = pad_lanes(jnp.concatenate([vec.reshape(device_count, -1) for vec in grads], axis=1))
+    dp_count = lax.axis_size("dp")
+    by_tensor = jnp.swapaxes(table.reshape(dp_count, -1, table.shape[1]), 0, 1)
+    summed = reduce_dp(reduce_level(by_tensor, "tensor", 1)).reshape(-1)
     own = []
     place = 0
     for vector in small:

time: 856 us -> 680 us (0.79)
  waiting for transfers between devices: 469 us -> 340 us
  blocking collectives: 125 us -> 0 us
  starting transfers between devices: 1.86 us -> 64.7 us
  local copies, waits for them, and re-layouts: 35.3 us -> 60.5 us
  matrix products: 95.5 us -> 76.9 us
  other arithmetic: 34.9 us -> 44 us
    ppermute x0 -> x48, waiting for transfers between devices: none -> 130 us  [the longest x18 76.4 us: gather_level(): part = lax.ppermute(values, axis, swap_pairs(count, unit, step))]
    reduce_scatter x4 -> x0, waiting for transfers between devices: 113 us -> none  [the longest x1 53.4 us: body(): lax.psum_scatter(contract_cols(hidden_act, proj_local).astype(jnp.bfloat1...]
    all_gather x3 -> x0, waiting for transfers between devices: 99.3 us -> none  [the longest x1 54.2 us: body(): group_top = lax.all_gather(out_grad, 'tensor', axis=0, tiled=True)]
    all_gather x2 -> x0, blocking collectives: 85.7 us -> none  [the longest x1 69.9 us: body(): lax.all_gather(pad_lanes(jnp.concatenate(small)[None, :]), ('dp', 'tensor...]
    ppermute x0 -> x48, starting transfers between devices: none -> 63.7 us  [the longest x21 36.9 us: reduce_level(): lax.ppermute(pick(values, group ^ step), axis, swap_pairs(count, unit, st...]
    all_gather x1, waiting for transfers between devices: 54.6 us -> 0.01 us  [body(): group_two = lax.all_gather(low_two, 'tensor', axis=0, tiled=True)]
    reduce_scatter x1, waiting for transfers between devices: 52 us -> 0.01 us  [body(): lax.psum_scatter(jnp.einsum('tcn,dcn->td', stacked, qkv_local, preferred_...]
    unnamed x1 -> x0, blocking collectives: 39.8 us -> none
  transfers between devices with their start and end apart: 15 -> 55, of which waited for: 12 -> 26; matrix products, arithmetic and copies ran while one was open for 12% -> 15% of each run, Pallas kernels for 5% -> 0%
where the time goes in v2:
time: 680 us; the launch traced here: 671 us
  waiting for transfers between devices  340 us (50%)
  matrix products  76.9 us (11%)
  Pallas kernels  69.9 us (10%)
  starting transfers between devices  64.7 us (10%)
  local copies, waits for them, and re-layouts  60.5 us (9%)
  other arithmetic  44 us (6%)
  between operations  15.5 us (2%)
    ppermute x18, waiting for transfers between devices, gather_level(): part = lax.ppermute(values, axis, swap_pairs(count, unit, step))  76.4 us
    reduce_scatter x1, waiting for transfers between devices, body(): lax.psum_scatter(contract_cols(low_pre, fc_local).astype(jnp.bfloat16), '...  64.5 us
    reduce_scatter x1, waiting for transfers between devices, body(): lax.psum_scatter(contract_cols(context, out_local).astype(jnp.bfloat16),...  52.4 us
    ppermute x21, waiting for transfers between devices, reduce_level(): lax.ppermute(pick(values, group ^ step), axis, swap_pairs(count, unit, st...  51.3 us
    all_gather x1, waiting for transfers between devices, body(): lax.all_gather(normed_one.astype(jnp.bfloat16), 'tensor', axis=0, tiled=T...  46.6 us
    all_gather x1, waiting for transfers between devices, body(): group_mid = lax.all_gather(low_mid, 'tensor', axis=0, tiled=True)  45.9 us
    pallas_call x1, Pallas kernels, attend_back(): pl.pallas_call(functools.partial(attend_back_kernel, heads, block), out_s...  44.2 us
    ppermute x21, starting transfers between devices, reduce_level(): lax.ppermute(pick(values, group ^ step), axis, swap_pairs(count, unit, st...  36.9 us
  transfers between devices with their start and end apart: 55, of which 26 were waited for; matrix products, arithmetic and copies ran while one was open for 15% of the time, Pallas kernels for 0%

profile of v2, /device:TPU:0, one launch (start us, length us, event | category | flops | bytes accessed | tf_op | source)
XLA Modules:
  0.0 671.2 jit_solution(13947056602008115931)
XLA Ops:
  8.0 5.4 concatenate.23
  37.6 5.5 collective-permute-done.8
  45.7 46.6 %all-gather.5.cloned.1.call-done = bf16[2048,1024]{1,0:T(8,128)(2,1)} async-done(((bf16[512,1024]{1,0:T(8,128)(2,1)}), bf16[2048,1024]{1,0:T(8,128)(2,1)}) %all-gather.5.cloned.1.call-update) | async-done | bytes 4194320 | tf_op jit(solution)/shard_map/all_gather | solution.py:367
  92.3 5.6 fusion.9
  109.7 25.7 %shard_map.254 = (f32[256,2048]{1,0:T(8,128)}, f32[4,1,2048]{2,1,0:T(1,128)S(1)}) custom-call(f32[4]{0:T(128)S(1)} %dynamic-slice_multiply_fusion.slope_ref, bf16[256,2048]{1,0:T(8,128)(2,1)S(1)} %fusion.94.qt_ref, bf16[2048,256]{1,0:T(8,128)(2,1)S(1)} %copy.47.k_ref, bf16[256,2048]{1,0:T(8,128)(2,1)S(1)} %copy-done.4, s32[1,2048]{1,0:T(1,128)S(1)} %bitcast.271, ...), custom_call_target="tpu_custom_call" | custom-call | flops 40000000000 | bytes 8000000 | tf_op jit(solution)/shard_map/pallas_call | solution.py:190
  140.8 52.4 %reduce-scatter.4.cloned.1.call-done = bf16[512,1024]{1,0:T(8,128)(2,1)} async-done(((bf16[2048,1024]{1,0:T(8,128)(2,1)}), bf16[512,1024]{1,0:T(8,128)(2,1)}) %reduce-scatter.4.cloned.1.call-update) | async-done | bytes 1048592 | tf_op jit(solution)/shard_map/reduce_scatter | solution.py:376
  215.3 7.2 %collective-permute-done.15 = bf16[128,1024]{1,0:T(8,128)(2,1)} collective-permute-done((bf16[128,1024]{1,0:T(8,128)(2,1)S(1)}, bf16[128,1024]{1,0:T(8,128)(2,1)}, u32[]{:S(2)}, u32[]{:S(2)}) %collective-permute-start.15) | collective-permute-done | bytes 262176 | tf_op jit(solution)/shard_map/ppermute | solution.py:270
  225.5 21.1 %collective-permute-done.16 = bf16[128,1024]{1,0:T(8,128)(2,1)S(1)} collective-permute-done((bf16[128,1024]{1,0:T(8,128)(2,1)S(1)}, bf16[128,1024]{1,0:T(8,128)(2,1)S(1)}, u32[]{:S(2)}, u32[]{:S(2)}) %collective-permute-start.16) | collective-permute-done | bytes 262176 | tf_op jit(solution)/shard_map/ppermute | solution.py:270
  255.8 14.8 %collective-permute-done.22 = bf16[512,1024]{1,0:T(8,128)(2,1)S(1)} collective-permute-done((bf16[512,1024]{1,0:T(8,128)(2,1)}, bf16[512,1024]{1,0:T(8,128)(2,1)S(1)}, u32[]{:S(2)}, u32[]{:S(2)}) %collective-permute-start.22) | collective-permute-done | bytes 1048608 | tf_op jit(solution)/shard_map/ppermute | solution.py:270
  271.6 22.9 %collective-permute-done.23 = bf16[512,1024]{1,0:T(8,128)(2,1)S(1)} collective-permute-done((bf16[512,1024]{1,0:T(8,128)(2,1)}, bf16[512,1024]{1,0:T(8,128)(2,1)S(1)}, u32[]{:S(2)}, u32[]{:S(2)}) %collective-permute-start.23) | collective-permute-done | bytes 1048608 | tf_op jit(solution)/shard_map/ppermute | solution.py:270
  302.6 7.1 %fusion.76 = f32[2048,1024]{1,0:T(8,128)S(1)} fusion(bf16[2048,1024]{1,0:T(8,128)(2,1)} %all-gather.9.cloned.1.call-done, bf16[1024,1024]{1,0:T(8,128)(2,1)} %bitcast.290), kind=kOutput, calls=%fused_computation.203 | convolution fusion | flops 4294967296 | bytes 14680064 | tf_op jit(solution)/shard_map/dot_general | solution.py:387
  309.7 10.5 %convert_reduce_fusion = (f32[1024]{0:T(1024)}, bf16[2048,1024]{1,0:T(8,128)(2,1)S(1)}) fusion(f32[2048,1024]{1,0:T(8,128)S(1)} %fusion.76, f32[1024]{0:T(1024)S(1)} %dynamic_slice.131, bf16[2048,1024]{1,0:T(8,128)(2,1)S(1)} %bitcast.276, bf16[1024,1024]{1,0:T(8,128)(2,1)S(1)} %bitcast.289), kind=kOutput, calls=%fused_computation.10 | convolution fusion | flops 4343200768 | bytes 18882560 | tf_op jit(solution)/shard_map/dot_general | solution.py:394
  322.2 6.3 convolution_convert_fusion.1
  329.0 9.9 %convolution_convert_fusion.2 = bf16[2048,1024]{1,0:T(8,128)(2,1)S(1)} fusion(bf16[1024,1024]{1,0:T(8,128)(2,1)} %bitcast.288, f32[2048,1024]{1,0:T(8,128)} %copy-done.46, f32[1024]{0:T(1024)S(1)} %dynamic_slice.131), kind=kOutput, calls=%fused_computation.19 | convolution fusion | flops 4318035968 | bytes 14684160 | tf_op jit(solution)/shard_map/dot_general | solution.py:35
  345.4 64.5 %reduce-scatter.6.cloned.1.call-done = bf16[512,1024]{1,0:T(8,128)(2,1)} async-done(((bf16[2048,1024]{1,0:T(8,128)(2,1)}), bf16[512,1024]{1,0:T(8,128)(2,1)}) %reduce-scatter.6.cloned.1.call-update) | async-done | bytes 1048592 | tf_op jit(solution)/shard_map/reduce_scatter | solution.py:405
  430.0 45.9 %all-gather.11.cloned.1.call-done = bf16[2048,1024]{1,0:T(8,128)(2,1)} async-done(((bf16[512,1024]{1,0:T(8,128)(2,1)}), bf16[2048,1024]{1,0:T(8,128)(2,1)}) %all-gather.11.cloned.1.call-update) | async-done | bytes 4194320 | tf_op jit(solution)/shard_map/all_gather | solution.py:418
  481.9 44.2 %shard_map.255 = (bf16[256,2048]{1,0:T(8,128)(2,1)S(1)}, bf16[2048,256]{1,0:T(8,128)(2,1)S(1)}, bf16[2048,256]{1,0:T(8,128)(2,1)S(1)}) custom-call(f32[4]{0:T(128)S(1)} %dynamic-slice_multiply_fusion.slope_ref, bf16[2048,256]{1,0:T(8,128)(2,1)S(1)} %copy-done.2, bf16[256,2048]{1,0:T(8,128)(2,1)S(1)} %fusion.94.qt_ref, bf16[2048,256]{1,0:T(8,128)(2,1)} %copy-done.1, ...), custom_call_target="tpu_custom_call" | custom-call | flops 80000000000 | bytes 16000000 | tf_op jit(solution)/shard_map/pallas_call | solution.py:215
  528.6 6.7 %bitcast_convert_fusion = bf16[2048,1024]{1,0:T(8,128)(2,1)} fusion(bf16[1024,3,256]{2,0,1:T(8,128)(2,1)} %all-gather.7.cloned.1.call-done, bf16[2048,1,256]{2,0,1:T(8,128)(2,1)S(1)} %bitcast.267, bf16[2048,1,256]{2,0,1:T(8,128)(2,1)S(1)} %bitcast.264, bf16[2048,1,256]{2,0,1:T(8,128)(2,1)S(1)} %bitcast.279), kind=kOutput, calls=%fused_computation.9 | convolution fusion | flops 3226468352 | bytes 8912896 | tf_op jit(solution)/shard_map/tcn,dcn->td/dot_general | solution.py:446
  535.4 9.7 %convolution_convert_fusion.4 = bf16[1024,1024]{1,0:T(8,128)(2,1)S(1)} fusion(bf16[2048,1024]{1,0:T(8,128)(2,1)} %bitcast.275, f32[2048,1024]{1,0:T(8,128)} %copy-done.46, f32[1024]{0:T(1024)S(1)} %dynamic_slice.131), kind=kOutput, calls=%fused_computation.72 | convolution fusion | flops 4316987392 | bytes 14684160 | tf_op jit(solution)/shard_map/dot_general | solution.py:29
  566.2 5.8 collective-permute-start.42
  572.9 22.4 %collective-permute-done.46 = bf16[128,1024]{1,0:T(8,128)(2,1)S(1)} collective-permute-done((bf16[128,1024]{1,0:T(8,128)(2,1)S(1)}, bf16[128,1024]{1,0:T(8,128)(2,1)S(1)}, u32[]{:S(2)}, u32[]{:S(2)}) %collective-permute-start.46) | collective-permute-done | bytes 262176 | tf_op jit(solution)/shard_map/ppermute | solution.py:299
  596.3 9.3 %collective-permute-done.42 = bf16[128,1024]{1,0:T(8,128)(2,1)S(1)} collective-permute-done((bf16[128,1024]{1,0:T(8,128)(2,1)S(1)}, bf16[128,1024]{1,0:T(8,128)(2,1)S(1)}, u32[]{:S(2)}, u32[]{:S(2)}) %collective-permute-start.42) | collective-permute-done | bytes 262176 | tf_op jit(solution)/shard_map/ppermute | solution.py:299
  647.4 4.9 collective-permute-start.30
  652.8 8.6 %collective-permute-done.34 = bf16[128,3,256]{2,0,1:T(8,128)(2,1)S(1)} collective-permute-done((bf16[128,3,256]{2,0,1:T(8,128)(2,1)S(1)}, bf16[128,3,256]{2,0,1:T(8,128)(2,1)S(1)}, u32[]{:S(2)}, u32[]{:S(2)}) %collective-permute-start.34) | collective-permute-done | bytes 196640 | tf_op jit(solution)/shard_map/ppermute | solution.py:299
  (338 shorter events, 192.7 us)
Async XLA Ops:
  7.2 38.5 %all-gather.7.cloned.1.call-start = ((), (), s32[]{:S(2)}) async-start(), calls=%async_computation.4 | async-start | bytes 1769472 | tf_op jit(solution)/shard_map/all_gather | solution.py:352
  7.9 84.4 %all-gather.5.cloned.1.call-start = ((), (), s32[]{:S(2)}) async-start(), calls=%async_computation.3 | async-start | bytes 5242880 | tf_op jit(solution)/shard_map/all_gather | solution.py:367
  33.2 159.9 %reduce-scatter.4.cloned.1.call-start = ((), (), s32[]{:S(2)}) async-start(), calls=%async_computation.5 | async-start | bytes 5242880 | tf_op jit(solution)/shard_map/reduce_scatter | solution.py:376
  140.3 162.3 %all-gather.9.cloned.1.call-start = ((), (), s32[]{:S(2)}) async-start(), calls=%async_computation.6 | async-start | bytes 5242880 | tf_op jit(solution)/shard_map/all_gather | solution.py:385
  197.1 212.9 %reduce-scatter.6.cloned.1.call-start = ((), (), s32[]{:S(2)}) async-start(), calls=%async_computation.7 | async-start | bytes 5242880 | tf_op jit(solution)/shard_map/reduce_scatter | solution.py:405
  198.7 54.9 %collective-permute-start.13 = (bf16[128,1024]{1,0:T(8,128)(2,1)}, bf16[128,1024]{1,0:T(8,128)(2,1)}, u32[]{:S(2)}, u32[]{:S(2)}) collective-permute-start(bf16[128,1024]{1,0:T(8,128)(2,1)} %param.24), channel_id=1, source_target_pairs={{0,24},{4,28},{8,16},{12,20},{16,8},{20,12},{24,0},{28,4},{1,25},{... | collective-permute-start | bytes 786440 | tf_op jit(solution)/shard_map/ppermute | solution.py:270
  201.1 50.8 %collective-permute-start.12 = (bf16[128,1024]{1,0:T(8,128)(2,1)}, bf16[128,1024]{1,0:T(8,128)(2,1)}, u32[]{:S(2)}, u32[]{:S(2)}) collective-permute-start(bf16[128,1024]{1,0:T(8,128)(2,1)} %param.24), channel_id=1, source_target_pairs={{0,16},{4,20},{8,24},{12,28},{16,0},{20,4},{24,8},{28,12},{1,17},{... | collective-permute-start | bytes 786440 | tf_op jit(solution)/shard_map/ppermute | solution.py:270
  201.1 21.4 %collective-permute-start.15 = (bf16[128,1024]{1,0:T(8,128)(2,1)S(1)}, bf16[128,1024]{1,0:T(8,128)(2,1)}, u32[]{:S(2)}, u32[]{:S(2)}) collective-permute-start(bf16[128,1024]{1,0:T(8,128)(2,1)S(1)} %copy-done.31), channel_id=1, source_target_pairs={{0,8},{4,12},{8,0},{12,4},{16,24},{20,28},{24,16},{28,20},{1,9},{5... | collective-permute-start | bytes 786440 | tf_op jit(solution)/shard_map/ppermute | solution.py:270
  203.1 45.7 %collective-permute-start.17 = (bf16[128,1024]{1,0:T(8,128)(2,1)S(1)}, bf16[128,1024]{1,0:T(8,128)(2,1)}, u32[]{:S(2)}, u32[]{:S(2)}) collective-permute-start(bf16[128,1024]{1,0:T(8,128)(2,1)S(1)} %copy-done.31), channel_id=1, source_target_pairs={{0,24},{4,28},{8,16},{12,20},{16,8},{20,12},{24,0},{28,4},{1,25},{... | collective-permute-start | bytes 786440 | tf_op jit(solution)/shard_map/ppermute | solution.py:270
  213.5 33.2 %collective-permute-start.16 = (bf16[128,1024]{1,0:T(8,128)(2,1)S(1)}, bf16[128,1024]{1,0:T(8,128)(2,1)S(1)}, u32[]{:S(2)}, u32[]{:S(2)}) collective-permute-start(bf16[128,1024]{1,0:T(8,128)(2,1)S(1)} %copy-done.31), channel_id=1, source_target_pairs={{0,16},{4,20},{8,24},{12,28},{16,0},{20,4},{24,8},{28,12},{1,17},{... | collective-permute-start | bytes 786440 | tf_op jit(solution)/shard_map/ppermute | solution.py:270
  222.5 48.0 %collective-permute-start.22 = (bf16[512,1024]{1,0:T(8,128)(2,1)}, bf16[512,1024]{1,0:T(8,128)(2,1)S(1)}, u32[]{:S(2)}, u32[]{:S(2)}) collective-permute-start(bf16[512,1024]{1,0:T(8,128)(2,1)} %param.29), channel_id=1, source_target_pairs={{0,1},{1,0},{2,3},{3,2},{4,5},{5,4},{6,7},{7,6},{8,9},{9,8},{10,11... | collective-permute-start | bytes 3145736 | tf_op jit(solution)/shard_map/ppermute | solution.py:270
  246.7 47.9 %collective-permute-start.23 = (bf16[512,1024]{1,0:T(8,128)(2,1)}, bf16[512,1024]{1,0:T(8,128)(2,1)S(1)}, u32[]{:S(2)}, u32[]{:S(2)}) collective-permute-start(bf16[512,1024]{1,0:T(8,128)(2,1)} %param.29), channel_id=1, source_target_pairs={{0,2},{1,3},{2,0},{3,1},{4,6},{5,7},{6,4},{7,5},{8,10},{9,11},{10,... | collective-permute-start | bytes 3145736 | tf_op jit(solution)/shard_map/ppermute | solution.py:270
  248.8 46.8 %collective-permute-start.24 = (bf16[512,1024]{1,0:T(8,128)(2,1)}, bf16[512,1024]{1,0:T(8,128)(2,1)S(1)}, u32[]{:S(2)}, u32[]{:S(2)}) collective-permute-start(bf16[512,1024]{1,0:T(8,128)(2,1)} %param.29), channel_id=1, source_target_pairs={{0,3},{1,2},{2,1},{3,0},{4,7},{5,6},{6,5},{7,4},{8,11},{9,10},{10,... | collective-permute-start | bytes 3145736 | tf_op jit(solution)/shard_map/ppermute | solution.py:270
  251.9 44.7 %collective-permute-start.18 = (bf16[4,128,1024]{2,1,0:T(8,128)(2,1)}, bf16[4,128,1024]{2,1,0:T(8,128)(2,1)S(1)}, u32[]{:S(2)}, u32[]{:S(2)}) collective-permute-start(bf16[4,128,1024]{2,1,0:T(8,128)(2,1)} %bitcast_dynamic-update-slice_fusion.4), channel_id=1, source_target_pairs={{0,4},{4,0},{8,12},{12,8},{16,20},{20,16},{24,28},{28,24},{1,5},{5... | collective-permute-start | bytes 3145736 | tf_op jit(solution)/shard_map/ppermute | solution.py:284
  255.3 44.4 %collective-permute-start.14 = (bf16[4,128,1024]{2,1,0:T(8,128)(2,1)}, bf16[4,128,1024]{2,1,0:T(8,128)(2,1)S(1)}, u32[]{:S(2)}, u32[]{:S(2)}) collective-permute-start(bf16[4,128,1024]{2,1,0:T(8,128)(2,1)} %bitcast_dynamic-update-slice_fusion.8), channel_id=1, source_target_pairs={{0,4},{4,0},{8,12},{12,8},{16,20},{20,16},{24,28},{28,24},{1,5},{5... | collective-permute-start | bytes 3145736 | tf_op jit(solution)/shard_map/ppermute | solution.py:284
  328.5 147.3 %all-gather.11.cloned.1.call-start = ((), (), s32[]{:S(2)}) async-start(), calls=%async_computation.8 | async-start | bytes 5242880 | tf_op jit(solution)/shard_map/all_gather | solution.py:418
  341.9 70.5 %collective-permute-start.19 = (bf16[512,1024]{1,0:T(8,128)(2,1)}, bf16[512,1024]{1,0:T(8,128)(2,1)}, u32[]{:S(2)}, u32[]{:S(2)}) collective-permute-start(bf16[512,1024]{1,0:T(8,128)(2,1)} %get-tuple-element.37), channel_id=1, source_target_pairs={{0,1},{1,0},{2,3},{3,2},{4,5},{5,4},{6,7},{7,6},{8,9},{9,8},{10,11... | collective-permute-start | bytes 3145736 | tf_op jit(solution)/shard_map/ppermute | solution.py:299
  343.4 73.6 %collective-permute-start.21 = (bf16[512,1024]{1,0:T(8,128)(2,1)}, bf16[512,1024]{1,0:T(8,128)(2,1)}, u32[]{:S(2)}, u32[]{:S(2)}) collective-permute-start(bf16[512,1024]{1,0:T(8,128)(2,1)} %get-tuple-element.38), channel_id=1, source_target_pairs={{0,3},{1,2},{2,1},{3,0},{4,7},{5,6},{6,5},{7,4},{8,11},{9,10},{10,... | collective-permute-start | bytes 3145736 | tf_op jit(solution)/shard_map/ppermute | solution.py:299
  343.7 73.2 %collective-permute-start.20 = (bf16[512,1024]{1,0:T(8,128)(2,1)}, bf16[512,1024]{1,0:T(8,128)(2,1)}, u32[]{:S(2)}, u32[]{:S(2)}) collective-permute-start(bf16[512,1024]{1,0:T(8,128)(2,1)} %get-tuple-element.39), channel_id=1, source_target_pairs={{0,2},{1,3},{2,0},{3,1},{4,6},{5,7},{6,4},{7,5},{8,10},{9,11},{10,... | collective-permute-start | bytes 3145736 | tf_op jit(solution)/shard_map/ppermute | solution.py:299
  422.7 203.3 %reduce-scatter.8.cloned.1.call-start = ((), (), s32[]{:S(2)}) async-start(), calls=%async_computation.9 | async-start | bytes 5242880 | tf_op jit(solution)/shard_map/reduce_scatter | solution.py:445
  560.0 35.3 %collective-permute-start.46 = (bf16[128,1024]{1,0:T(8,128)(2,1)S(1)}, bf16[128,1024]{1,0:T(8,128)(2,1)S(1)}, u32[]{:S(2)}, u32[]{:S(2)}) collective-permute-start(bf16[128,1024]{1,0:T(8,128)(2,1)S(1)} %get-tuple-element.49), channel_id=1, source_target_pairs={{0,16},{4,20},{8,24},{12,28},{16,0},{20,4},{24,8},{28,12},{1,17},{... | collective-permute-start | bytes 786440 | tf_op jit(solution)/shard_map/ppermute | solution.py:299
  561.8 34.5 %collective-permute-start.41 = (bf16[128,1024]{1,0:T(8,128)(2,1)S(1)}, bf16[128,1024]{1,0:T(8,128)(2,1)S(1)}, u32[]{:S(2)}, u32[]{:S(2)}) collective-permute-start(bf16[128,1024]{1,0:T(8,128)(2,1)S(1)} %get-tuple-element.50), channel_id=1, source_target_pairs={{0,8},{4,12},{8,0},{12,4},{16,24},{20,28},{24,16},{28,20},{1,9},{5... | collective-permute-start | bytes 786440 | tf_op jit(solution)/shard_map/ppermute | solution.py:299
  563.8 32.4 %collective-permute-start.43 = (bf16[128,1024]{1,0:T(8,128)(2,1)S(1)}, bf16[128,1024]{1,0:T(8,128)(2,1)S(1)}, u32[]{:S(2)}, u32[]{:S(2)}) collective-permute-start(bf16[128,1024]{1,0:T(8,128)(2,1)S(1)} %get-tuple-element.51), channel_id=1, source_target_pairs={{0,24},{4,28},{8,16},{12,20},{16,8},{20,12},{24,0},{28,4},{1,25},{... | collective-permute-start | bytes 786440 | tf_op jit(solution)/shard_map/ppermute | solution.py:299
  566.2 39.3 %collective-permute-start.42 = (bf16[128,1024]{1,0:T(8,128)(2,1)S(1)}, bf16[128,1024]{1,0:T(8,128)(2,1)S(1)}, u32[]{:S(2)}, u32[]{:S(2)}) collective-permute-start(bf16[128,1024]{1,0:T(8,128)(2,1)S(1)} %get-tuple-element.52), channel_id=1, source_target_pairs={{0,16},{4,20},{8,24},{12,28},{16,0},{20,4},{24,8},{28,12},{1,17},{... | collective-permute-start | bytes 786440 | tf_op jit(solution)/shard_map/ppermute | solution.py:299
  (78 other events, 752.6 us)
Sparse Core Ops, SparseCore 0:
  9.6 27.9 all-gather.6
  40.0 52.2 all-gather.4
  140.4 52.6 reduce-scatter.3
  197.2 75.0 all-gather.8
  328.7 81.2 reduce-scatter.5
  422.8 52.9 all-gather.10
  535.4 52.6 reduce-scatter.7
